TPU v7x, 256 devices: a whole 4x4x8 slice. The times are simulated.
256 devices in a mesh: dp: 32 (over y_lo, z, core), ctx: 8 (over x, y_hi).
Axes of the slice: x: 4, y: 4 (y_hi: 2, y_lo: 2; y = y_hi * 2 + y_lo), z: 8, core: 2. Of those that a mesh axis runs over, the one named last changes fastest.
Arguments:
- history: bfloat16 [32, 1024, 1024], P('dp', 'ctx'), may hold values from -6 to 6
- cotangent: bfloat16 [32, 1024, 1024], P('dp', 'ctx'), may hold values from -6 to 6
- lengths: int32 [32, 3], P('dp'), may hold values from 1 to 819, as said below
- w_proj: bfloat16 [1024, 2048], replicated, may hold values from -0.1875 to 0.1875
- w_out: bfloat16 [512, 1024], replicated, may hold values from -0.25 to 0.25
Outputs:
- d_history: bfloat16 [32, 1024, 1024], P('dp', 'ctx')
- grad_proj: bfloat16 [1024, 2048], replicated
- grad_out: bfloat16 [512, 1024], replicated
Inputs may be any that keep to these rules, and one draw needn't show every extreme that they name: Each batch's lengths sum to 1024; the first history of each batch is its longest, with exactly 819 events.
All inputs are finite; a program needn't handle non-finite values.
Results may differ from a plain program's by a relative error of at most 0.0092.
Values may be sent and summed in bfloat16 or wider, within the bound.
A program may use at most 128 MiB of HBM per device.

v0:
```python
import jax
import jax.numpy as jnp
from jax import lax
from jax.sharding import PartitionSpec as P

HEAD_DIM = 128


EPSILON = 1e-05


def passed_along(array, axis, by):
    devices = lax.axis_size(axis)
    return lax.ppermute(array, axis, [(i, (i + by) % devices) for i in range(devices)])


def silu_grad(values):
    sigmoid = jax.nn.sigmoid(values)
    return sigmoid * (1.0 + values * (1.0 - sigmoid))


def normalize(values):
    average = jnp.mean(values, axis=-1, keepdims=True)
    centred = values - average
    variance = jnp.mean(centred * centred, axis=-1, keepdims=True)
    inv_scale = lax.rsqrt(variance + EPSILON)
    return (centred * inv_scale, inv_scale)


def norm_back(grad, normed, inv_scale):
    first = jnp.mean(grad, axis=-1, keepdims=True)
    second = jnp.mean(grad * normed, axis=-1, keepdims=True)
    return inv_scale * (grad - first - normed * second)


def segment_of(positions, history_ends):
    return jnp.sum((positions[:, None] >= history_ends[None, :]).astype(jnp.int32), axis=1)


def on_device(history, cotangent, lengths, w_proj, w_out):
    tokens_in = history[0]
    cot_rows = cotangent[0]
    row_count = tokens_in.shape[0]
    inner_width = w_out.shape[0]
    head_count = inner_width // HEAD_DIM
    score_scale = HEAD_DIM ** (-0.5)
    cycle_size = lax.axis_size("ctx")
    position = lax.axis_index("ctx")
    history_ends = jnp.cumsum(lengths[0])
    local_pos = jnp.arange(row_count, dtype=jnp.int32)
    query_pos = position * row_count + local_pos
    query_seg = segment_of(query_pos, history_ends)

    def block_allowed(source):
        key_pos = source * row_count + local_pos
        key_seg = segment_of(key_pos, history_ends)
        return (query_seg[:, None] == key_seg[None, :]) & (key_pos[None, :] >= query_pos[:, None])

    x_norm, x_scale = normalize(tokens_in.astype(jnp.float32))
    normed = x_norm.astype(jnp.bfloat16)
    pre = jnp.dot(normed, w_proj, preferred_element_type=jnp.float32)
    proj = jax.nn.silu(pre).astype(jnp.bfloat16)
    gate_u = proj[:, :inner_width].astype(jnp.float32)
    value_heads = proj[:, inner_width : 2 * inner_width].reshape(row_count, head_count, HEAD_DIM)
    query_heads = proj[:, 2 * inner_width : 3 * inner_width].reshape(
        row_count, head_count, HEAD_DIM
    )
    key_heads = proj[:, 3 * inner_width :].reshape(row_count, head_count, HEAD_DIM)

    def block_logits(keys_block, source):
        logits = (
            jnp.einsum("qhd,khd->hqk", query_heads, keys_block, preferred_element_type=jnp.float32)
            * score_scale
        )
        return (logits, block_allowed(source))

    def forward_block(summed, keys_block, values_block, source):
        logits, allowed = block_logits(keys_block, source)
        weights = jnp.where(allowed[None], jax.nn.silu(logits), 0.0).astype(jnp.bfloat16)
        return summed + jnp.einsum(
            "hqk,khd->qhd", weights, values_block, preferred_element_type=jnp.float32
        )

    zero_heads = jnp.zeros((row_count, head_count, HEAD_DIM), jnp.float32)
    attn_start = forward_block(zero_heads, key_heads, value_heads, position)

    def forward_turn(step_index, loop_state):
        summed, keys_block, values_block = loop_state
        keys_block, values_block = passed_along((keys_block, values_block), "ctx", 1)
        source = (position - step_index) % cycle_size
        return (forward_block(summed, keys_block, values_block, source), keys_block, values_block)

    attn, _, _ = lax.fori_loop(1, cycle_size, forward_turn, (attn_start, key_heads, value_heads))
    a_norm, a_scale = normalize(attn.reshape(row_count, inner_width))
    gated = (a_norm * gate_u).astype(jnp.bfloat16)
    grad_o = jnp.dot(gated.T, cot_rows, preferred_element_type=jnp.float32)
    d_gated = jnp.dot(cot_rows, w_out.T, preferred_element_type=jnp.float32)
    d_u = d_gated * a_norm
    d_attn = norm_back(d_gated * gate_u, a_norm, a_scale).astype(jnp.bfloat16)
    d_heads = d_attn.reshape(row_count, head_count, HEAD_DIM)

    def backward_block(partial_value, keys_block, values_block, source):
        d_query, d_keys, d_value = partial_value
        logits, allowed = block_logits(keys_block, source)
        weights = jnp.where(allowed[None], jax.nn.silu(logits), 0.0).astype(jnp.bfloat16)
        d_weights = jnp.einsum(
            "qhd,khd->hqk", d_heads, values_block, preferred_element_type=jnp.float32
        )
        d_logits = jnp.where(allowed[None], d_weights * silu_grad(logits), 0.0).astype(jnp.bfloat16)
        d_query = d_query + jnp.einsum(
            "hqk,khd->qhd", d_logits, keys_block, preferred_element_type=jnp.float32
        )
        d_keys = d_keys + jnp.einsum(
            "hqk,qhd->khd", d_logits, query_heads, preferred_element_type=jnp.float32
        )
        d_value = d_value + jnp.einsum(
            "hqk,qhd->khd", weights, d_heads, preferred_element_type=jnp.float32
        )
        return (d_query, d_keys, d_value)

    first = backward_block((zero_heads, zero_heads, zero_heads), key_heads, value_heads, position)

    def backward_turn(step_index, loop_state):
        d_query, keys_block, values_block, d_keys, d_value = loop_state
        keys_block, values_block = passed_along((keys_block, values_block), "ctx", 1)
        d_keys, d_value = passed_along((d_keys, d_value), "ctx", 1)
        source = (position - step_index) % cycle_size
        d_query, d_keys, d_value = backward_block(
            (d_query, d_keys, d_value), keys_block, values_block, source
        )
        return (d_query, keys_block, values_block, d_keys, d_value)

    d_query, _, _, d_keys, d_value = lax.fori_loop(
        1, cycle_size, backward_turn, (first[0], key_heads, value_heads, first[1], first[2])
    )
    d_keys, d_value = passed_along((d_keys, d_value), "ctx", 1)
    d_proj = jnp.concatenate(
        [
            d_u,
            d_value.reshape(row_count, inner_width),
            d_query.reshape(row_count, inner_width) * score_scale,
            d_keys.reshape(row_count, inner_width) * score_scale,
        ],
        axis=1,
    )
    d_pre = (d_proj * silu_grad(pre)).astype(jnp.bfloat16)
    grad_p = jnp.dot(normed.T, d_pre, preferred_element_type=jnp.float32)
    d_normed = jnp.dot(d_pre, w_proj.T, preferred_element_type=jnp.float32)
    d_rows = (cot_rows.astype(jnp.float32) + norm_back(d_normed, x_norm, x_scale)).astype(
        jnp.bfloat16
    )
    flattened = jnp.concatenate([grad_p.reshape(-1), grad_o.reshape(-1)])
    shard_sum = lax.psum_scatter(flattened, "ctx", scatter_dimension=0, tiled=True)
    shard_sum = lax.psum(shard_sum, "dp")
    combined = lax.all_gather(shard_sum.astype(jnp.bfloat16), "ctx", axis=0, tiled=True)
    proj_count = grad_p.size
    return (
        d_rows[None],
        combined[:proj_count].reshape(w_proj.shape),
        combined[proj_count:].reshape(w_out.shape),
    )


def solution(mesh):
    in_specs = (P("dp", "ctx", None), P("dp", "ctx", None), P("dp", None), P(), P())
    out_specs = (P("dp", "ctx", None), P(), P())
    return jax.shard_map(
        on_device, mesh=mesh, in_specs=in_specs, out_specs=out_specs, check_vma=False
    )
```

profile of v0, /device:TPU:1, one launch (start us, length us, event | category | flops | bytes accessed | tf_op | source)
XLA Modules:
  0.0 933.8 jit_solution(11678507835796109093)
XLA Ops:
  9.6 4.1 multiply_convert_fusion
  16.0 70.3 %while.44 = (s32[]{:T(128)}, f32[128,4,128]{2,0,1:T(8,128)S(1)}, bf16[128,4,128]{2,0,1:T(8,128)(2,1)S(1)}, bf16[128,4,128]{2,0,1:T(8,128)(2,1)S(1)}, s32[128]{0:...) while((s32[]{:T(128)}, f32[128,4,128]{2,0,1:T(8,128)S(1)}, ...), condition=%wide.region_6.7_spmd.clone, body=%wide.region_4.6_spmd.clone.sunk | while | flops 34129168 | bytes 2527598 | solution.py:93
  16.0 3.8 collective-permute-start
  21.6 7.4 collective-permute-done.1
  31.3 7.9 collective-permute-done.1
  39.7 1.6 collective-permute-start.1
  42.0 6.4 collective-permute-done.1
  50.8 7.0 collective-permute-done.1
  59.2 7.9 collective-permute-done.1
  68.6 7.9 collective-permute-done.1
  77.9 8.0 collective-permute-done.1
  87.5 1.3 fusion.27
  91.5 145.6 %while.45 = (s32[]{:T(128)}, f32[128,4,128]{2,0,1:T(8,128)S(1)}, bf16[128,4,128]{2,0,1:T(8,128)(2,1)S(1)}, bf16[128,4,128]{2,0,1:T(8,128)(2,1)S(1)}, f32[128,4,1...) while((s32[]{:T(128)}, f32[128,4,128]{2,0,1:T(8,128)S(1)}, ...), condition=%wide.region_13.14_spmd.clone, body=%wide.region_11.13_spmd.clone.sunk | while | flops 85247232 | bytes 7918066 | solution.py:133
  92.6 2.3 collective-permute-start.5
  95.7 4.7 collective-permute-done.3
  102.0 1.2 collective-permute-done.4
  103.5 2.7 collective-permute-done.5
  106.1 1.2 fusion.113
  107.5 1.4 collective-permute-start.3
  109.8 3.3 collective-permute-start.5
  113.9 3.8 collective-permute-done.3
  119.2 1.2 collective-permute-done.4
  120.7 2.7 collective-permute-done.5
  123.4 1.2 fusion.113
  124.7 1.6 collective-permute-start.3
  126.4 2.2 collective-permute-start.4
  128.6 2.8 collective-permute-start.5
  132.2 4.6 collective-permute-done.3
  138.4 1.9 collective-permute-done.4
  140.5 2.7 collective-permute-done.5
  143.2 1.2 fusion.113
  144.5 3.3 collective-permute-start.3
  148.0 2.3 collective-permute-start.5
  151.2 4.4 collective-permute-done.3
  157.2 4.1 collective-permute-done.4
  161.6 4.4 collective-permute-done.5
  166.0 1.2 fusion.113
  167.3 3.1 collective-permute-start.3
  171.5 7.4 collective-permute-done.3
  180.4 4.0 collective-permute-done.4
  184.7 5.5 collective-permute-done.5
  190.2 1.2 fusion.113
  191.5 1.6 collective-permute-start.3
  194.1 8.1 collective-permute-done.3
  203.7 4.0 collective-permute-done.4
  208.0 5.5 collective-permute-done.5
  213.5 1.2 fusion.113
  215.9 8.6 collective-permute-done.3
  226.1 4.0 collective-permute-done.4
  230.4 5.5 collective-permute-done.5
  237.9 1.3 convolution_bitcast_fusion.5
  239.7 7.6 collective-permute-done.7
  247.3 5.6 collective-permute-done.6
  253.0 1.4 convolution_bitcast_fusion.4
  254.4 2.0 copy.93
  256.4 8.1 pad_maximum_fusion
  266.4 440.3 %all-reduce.4.cloned.1.call-done = f32[2621440]{0:T(1024)} async-done(((f32[2621440]{0:T(1024)}), f32[2621440]{0:T(1024)}) %all-reduce.4.cloned.1.call-update) | async-done | bytes 10485776
  706.7 1.4 dynamic-slice.1
  708.1 116.8 %all-reduce.5 = bf16[327680]{0:T(1024)(128)(2,1)} all-reduce(f32[327680]{0:T(1024)S(1)} %dynamic-slice.1), channel_id=1, replica_groups=mesh['dp'=32,'ctx'=8] {'dp'}, use_global_device_ids=true, to_apply=%region_17.18 | all-reduce | flops 327680 | bytes 1966080 | tf_op jit(solution)/shard_map/psum | solution.py:154
  825.0 4.0 fusion.56
  830.0 84.6 %all-gather.2.cloned.1.call-done = bf16[2621440]{0:T(1024)(128)(2,1)} async-done(((bf16[327680]{0:T(1024)(128)(2,1)}), bf16[2621440]{0:T(1024)(128)(2,1)}) %all-gather.2.cloned.1.call-update) | async-done | bytes 5242896 | tf_op jit(solution)/shard_map/all_gather | solution.py:155
  914.5 3.7 slice.50
  918.3 7.4 slice.43
  925.7 1.3 slice.45
  (248 shorter events, 46.3 us)
Async XLA Ops:
  7.2 79.5 %copy-start = (bf16[512,1024]{1,0:T(8,128)(2,1)S(1)}, bf16[512,1024]{1,0:T(8,128)(2,1)}, u32[]{:S(2)}) copy-start(bf16[512,1024]{1,0:T(8,128)(2,1)} %param.13) | copy-start | bytes 3145732
  7.2 699.6 %all-reduce.4.cloned.1.call-start = ((), (), s32[]{:S(2)}) async-start(), calls=%async_computation.1 | async-start | bytes 20971520
  9.6 4.4 copy-start.14
  16.0 70.6 %copy-start.3 = (bf16[1,128,1024]{2,1,0:T(8,128)(2,1)S(1)}, bf16[1,128,1024]{2,1,0:T(8,128)(2,1)}, u32[]{:S(2)}) copy-start(bf16[1,128,1024]{2,1,0:T(8,128)(2,1)} %param.10) | copy-start | bytes 786436
  16.0 13.0 %collective-permute-start = (bf16[128,4,128]{2,0,1:T(8,128)(2,1)S(1)}, bf16[128,4,128]{2,0,1:T(8,128)(2,1)S(1)}, u32[]{:S(2)}, u32[]{:S(2)}) collective-permute-start(bf16[128,4,128]{2,0,1:T(8,128)(2,1)S(1)} %get-tuple-element.882), channel_id=1, source_target_pairs={{0,1},{1,2},{2,3},{3,4},{4,5},{5,6},{6,7},{7,0},{8,9},{9,10},{10,1... | collective-permute-start | bytes 393224 | tf_op jit(solution)/shard_map/while/body/eval_jaxpr/ppermute | solution.py:14
  19.9 9.1 collective-permute-start.1
  29.4 9.7 %collective-permute-start = (bf16[128,4,128]{2,0,1:T(8,128)(2,1)S(1)}, bf16[128,4,128]{2,0,1:T(8,128)(2,1)S(1)}, u32[]{:S(2)}, u32[]{:S(2)}) collective-permute-start(bf16[128,4,128]{2,0,1:T(8,128)(2,1)S(1)} %get-tuple-element.882), channel_id=1, source_target_pairs={{0,1},{1,2},{2,3},{3,4},{4,5},{5,6},{6,7},{7,0},{8,9},{9,10},{10,1... | collective-permute-start | bytes 393224 | tf_op jit(solution)/shard_map/while/body/eval_jaxpr/ppermute | solution.py:14
  29.5 9.6 %collective-permute-start.1 = (bf16[128,4,128]{2,0,1:T(8,128)(2,1)S(1)}, bf16[128,4,128]{2,0,1:T(8,128)(2,1)S(1)}, u32[]{:S(2)}, u32[]{:S(2)}) collective-permute-start(bf16[128,4,128]{2,0,1:T(8,128)(2,1)S(1)} %get-tuple-element.881), channel_id=1, source_target_pairs={{0,1},{1,2},{2,3},{3,4},{4,5},{5,6},{6,7},{7,0},{8,9},{9,10},{10,1... | collective-permute-start | bytes 393224 | tf_op jit(solution)/shard_map/while/body/eval_jaxpr/ppermute | solution.py:14
  39.6 8.9 collective-permute-start
  39.7 8.8 collective-permute-start.1
  48.9 8.9 collective-permute-start
  49.0 8.8 collective-permute-start.1
  58.2 8.9 collective-permute-start
  58.3 8.8 collective-permute-start.1
  67.6 8.9 collective-permute-start
  67.7 8.8 collective-permute-start.1
  76.9 9.0 collective-permute-start
  77.0 8.9 collective-permute-start.1
  86.3 2.9 copy-start.12
  86.7 4.4 copy-start.13
  87.4 165.5 %copy-start.7 = (f32[128,512]{1,0:T(8,128)}, f32[128,512]{1,0:T(8,128)S(1)}, u32[]{:S(2)}) copy-start(f32[128,512]{1,0:T(8,128)S(1)} %get-tuple-element.722) | copy-start | bytes 786436
  91.5 9.1 collective-permute-start.2
  91.6 8.8 collective-permute-start.3
  91.7 11.5 %collective-permute-start.4 = (f32[128,4,128]{2,0,1:T(8,128)S(1)}, f32[128,4,128]{2,0,1:T(8,128)S(1)}, u32[]{:S(2)}, u32[]{:S(2)}) collective-permute-start(f32[128,4,128]{2,0,1:T(8,128)S(1)} %get-tuple-element.928), channel_id=1, source_target_pairs={{0,1},{1,2},{2,3},{3,4},{4,5},{5,6},{6,7},{7,0},{8,9},{9,10},{10,1... | collective-permute-start | bytes 786440 | tf_op jit(solution)/shard_map/while/body/eval_jaxpr/ppermute | solution.py:14
  92.6 13.5 %collective-permute-start.5 = (f32[128,4,128]{2,0,1:T(8,128)S(1)}, f32[128,4,128]{2,0,1:T(8,128)}, u32[]{:S(2)}, u32[]{:S(2)}) collective-permute-start(f32[128,4,128]{2,0,1:T(8,128)S(1)} %get-tuple-element.929), channel_id=1, source_target_pairs={{0,1},{1,2},{2,3},{3,4},{4,5},{5,6},{6,7},{7,0},{8,9},{9,10},{10,1... | collective-permute-start | bytes 786440 | tf_op jit(solution)/shard_map/while/body/eval_jaxpr/ppermute | solution.py:14
  94.9 11.2 %copy-start.10 = (bf16[128,4,128]{2,0,1:T(8,128)(2,1)S(1)}, bf16[128,4,128]{2,0,1:T(8,128)(2,1)}, u32[]{:S(2)}) copy-start(bf16[128,4,128]{2,0,1:T(8,128)(2,1)} %get-tuple-element.950) | copy-start | bytes 393220 | tf_op jit(solution)/shard_map/while
  107.4 10.5 %collective-permute-start.2 = (bf16[128,4,128]{2,0,1:T(8,128)(2,1)S(1)}, bf16[128,4,128]{2,0,1:T(8,128)(2,1)S(1)}, u32[]{:S(2)}, u32[]{:S(2)}) collective-permute-start(bf16[128,4,128]{2,0,1:T(8,128)(2,1)S(1)} %get-tuple-element.927), channel_id=1, source_target_pairs={{0,1},{1,2},{2,3},{3,4},{4,5},{5,6},{6,7},{7,0},{8,9},{9,10},{10,1... | collective-permute-start | bytes 393224 | tf_op jit(solution)/shard_map/while/body/eval_jaxpr/ppermute | solution.py:14
  107.5 10.2 %collective-permute-start.3 = (bf16[128,4,128]{2,0,1:T(8,128)(2,1)S(1)}, bf16[128,4,128]{2,0,1:T(8,128)(2,1)S(1)}, u32[]{:S(2)}, u32[]{:S(2)}) collective-permute-start(bf16[128,4,128]{2,0,1:T(8,128)(2,1)S(1)} %get-tuple-element.926), channel_id=1, source_target_pairs={{0,1},{1,2},{2,3},{3,4},{4,5},{5,6},{6,7},{7,0},{8,9},{9,10},{10,1... | collective-permute-start | bytes 393224 | tf_op jit(solution)/shard_map/while/body/eval_jaxpr/ppermute | solution.py:14
  108.9 11.6 %collective-permute-start.4 = (f32[128,4,128]{2,0,1:T(8,128)S(1)}, f32[128,4,128]{2,0,1:T(8,128)S(1)}, u32[]{:S(2)}, u32[]{:S(2)}) collective-permute-start(f32[128,4,128]{2,0,1:T(8,128)S(1)} %get-tuple-element.928), channel_id=1, source_target_pairs={{0,1},{1,2},{2,3},{3,4},{4,5},{5,6},{6,7},{7,0},{8,9},{9,10},{10,1... | collective-permute-start | bytes 786440 | tf_op jit(solution)/shard_map/while/body/eval_jaxpr/ppermute | solution.py:14
  109.8 13.6 %collective-permute-start.5 = (f32[128,4,128]{2,0,1:T(8,128)S(1)}, f32[128,4,128]{2,0,1:T(8,128)}, u32[]{:S(2)}, u32[]{:S(2)}) collective-permute-start(f32[128,4,128]{2,0,1:T(8,128)S(1)} %get-tuple-element.929), channel_id=1, source_target_pairs={{0,1},{1,2},{2,3},{3,4},{4,5},{5,6},{6,7},{7,0},{8,9},{9,10},{10,1... | collective-permute-start | bytes 786440 | tf_op jit(solution)/shard_map/while/body/eval_jaxpr/ppermute | solution.py:14
  113.1 10.3 %copy-start.10 = (bf16[128,4,128]{2,0,1:T(8,128)(2,1)S(1)}, bf16[128,4,128]{2,0,1:T(8,128)(2,1)}, u32[]{:S(2)}) copy-start(bf16[128,4,128]{2,0,1:T(8,128)(2,1)} %get-tuple-element.950) | copy-start | bytes 393220 | tf_op jit(solution)/shard_map/while
  124.6 12.4 %collective-permute-start.2 = (bf16[128,4,128]{2,0,1:T(8,128)(2,1)S(1)}, bf16[128,4,128]{2,0,1:T(8,128)(2,1)S(1)}, u32[]{:S(2)}, u32[]{:S(2)}) collective-permute-start(bf16[128,4,128]{2,0,1:T(8,128)(2,1)S(1)} %get-tuple-element.927), channel_id=1, source_target_pairs={{0,1},{1,2},{2,3},{3,4},{4,5},{5,6},{6,7},{7,0},{8,9},{9,10},{10,1... | collective-permute-start | bytes 393224 | tf_op jit(solution)/shard_map/while/body/eval_jaxpr/ppermute | solution.py:14
  124.7 12.1 %collective-permute-start.3 = (bf16[128,4,128]{2,0,1:T(8,128)(2,1)S(1)}, bf16[128,4,128]{2,0,1:T(8,128)(2,1)S(1)}, u32[]{:S(2)}, u32[]{:S(2)}) collective-permute-start(bf16[128,4,128]{2,0,1:T(8,128)(2,1)S(1)} %get-tuple-element.926), channel_id=1, source_target_pairs={{0,1},{1,2},{2,3},{3,4},{4,5},{5,6},{6,7},{7,0},{8,9},{9,10},{10,1... | collective-permute-start | bytes 393224 | tf_op jit(solution)/shard_map/while/body/eval_jaxpr/ppermute | solution.py:14
  126.4 13.9 %collective-permute-start.4 = (f32[128,4,128]{2,0,1:T(8,128)S(1)}, f32[128,4,128]{2,0,1:T(8,128)S(1)}, u32[]{:S(2)}, u32[]{:S(2)}) collective-permute-start(f32[128,4,128]{2,0,1:T(8,128)S(1)} %get-tuple-element.928), channel_id=1, source_target_pairs={{0,1},{1,2},{2,3},{3,4},{4,5},{5,6},{6,7},{7,0},{8,9},{9,10},{10,1... | collective-permute-start | bytes 786440 | tf_op jit(solution)/shard_map/while/body/eval_jaxpr/ppermute | solution.py:14
  128.6 14.6 %collective-permute-start.5 = (f32[128,4,128]{2,0,1:T(8,128)S(1)}, f32[128,4,128]{2,0,1:T(8,128)}, u32[]{:S(2)}, u32[]{:S(2)}) collective-permute-start(f32[128,4,128]{2,0,1:T(8,128)S(1)} %get-tuple-element.929), channel_id=1, source_target_pairs={{0,1},{1,2},{2,3},{3,4},{4,5},{5,6},{6,7},{7,0},{8,9},{9,10},{10,1... | collective-permute-start | bytes 786440 | tf_op jit(solution)/shard_map/while/body/eval_jaxpr/ppermute | solution.py:14
  131.4 11.8 %copy-start.10 = (bf16[128,4,128]{2,0,1:T(8,128)(2,1)S(1)}, bf16[128,4,128]{2,0,1:T(8,128)(2,1)}, u32[]{:S(2)}) copy-start(bf16[128,4,128]{2,0,1:T(8,128)(2,1)} %get-tuple-element.950) | copy-start | bytes 393220 | tf_op jit(solution)/shard_map/while
  144.4 11.4 %collective-permute-start.2 = (bf16[128,4,128]{2,0,1:T(8,128)(2,1)S(1)}, bf16[128,4,128]{2,0,1:T(8,128)(2,1)S(1)}, u32[]{:S(2)}, u32[]{:S(2)}) collective-permute-start(bf16[128,4,128]{2,0,1:T(8,128)(2,1)S(1)} %get-tuple-element.927), channel_id=1, source_target_pairs={{0,1},{1,2},{2,3},{3,4},{4,5},{5,6},{6,7},{7,0},{8,9},{9,10},{10,1... | collective-permute-start | bytes 393224 | tf_op jit(solution)/shard_map/while/body/eval_jaxpr/ppermute | solution.py:14
  144.5 11.1 %collective-permute-start.3 = (bf16[128,4,128]{2,0,1:T(8,128)(2,1)S(1)}, bf16[128,4,128]{2,0,1:T(8,128)(2,1)S(1)}, u32[]{:S(2)}, u32[]{:S(2)}) collective-permute-start(bf16[128,4,128]{2,0,1:T(8,128)(2,1)S(1)} %get-tuple-element.926), channel_id=1, source_target_pairs={{0,1},{1,2},{2,3},{3,4},{4,5},{5,6},{6,7},{7,0},{8,9},{9,10},{10,1... | collective-permute-start | bytes 393224 | tf_op jit(solution)/shard_map/while/body/eval_jaxpr/ppermute | solution.py:14
  147.8 13.5 %collective-permute-start.4 = (f32[128,4,128]{2,0,1:T(8,128)S(1)}, f32[128,4,128]{2,0,1:T(8,128)S(1)}, u32[]{:S(2)}, u32[]{:S(2)}) collective-permute-start(f32[128,4,128]{2,0,1:T(8,128)S(1)} %get-tuple-element.928), channel_id=1, source_target_pairs={{0,1},{1,2},{2,3},{3,4},{4,5},{5,6},{6,7},{7,0},{8,9},{9,10},{10,1... | collective-permute-start | bytes 786440 | tf_op jit(solution)/shard_map/while/body/eval_jaxpr/ppermute | solution.py:14
  148.0 17.9 %collective-permute-start.5 = (f32[128,4,128]{2,0,1:T(8,128)S(1)}, f32[128,4,128]{2,0,1:T(8,128)}, u32[]{:S(2)}, u32[]{:S(2)}) collective-permute-start(f32[128,4,128]{2,0,1:T(8,128)S(1)} %get-tuple-element.929), channel_id=1, source_target_pairs={{0,1},{1,2},{2,3},{3,4},{4,5},{5,6},{6,7},{7,0},{8,9},{9,10},{10,1... | collective-permute-start | bytes 786440 | tf_op jit(solution)/shard_map/while/body/eval_jaxpr/ppermute | solution.py:14
  150.3 15.6 %copy-start.10 = (bf16[128,4,128]{2,0,1:T(8,128)(2,1)S(1)}, bf16[128,4,128]{2,0,1:T(8,128)(2,1)}, u32[]{:S(2)}) copy-start(bf16[128,4,128]{2,0,1:T(8,128)(2,1)} %get-tuple-element.950) | copy-start | bytes 393220 | tf_op jit(solution)/shard_map/while
  167.2 11.8 %collective-permute-start.2 = (bf16[128,4,128]{2,0,1:T(8,128)(2,1)S(1)}, bf16[128,4,128]{2,0,1:T(8,128)(2,1)S(1)}, u32[]{:S(2)}, u32[]{:S(2)}) collective-permute-start(bf16[128,4,128]{2,0,1:T(8,128)(2,1)S(1)} %get-tuple-element.927), channel_id=1, source_target_pairs={{0,1},{1,2},{2,3},{3,4},{4,5},{5,6},{6,7},{7,0},{8,9},{9,10},{10,1... | collective-permute-start | bytes 393224 | tf_op jit(solution)/shard_map/while/body/eval_jaxpr/ppermute | solution.py:14
  167.3 11.5 %collective-permute-start.3 = (bf16[128,4,128]{2,0,1:T(8,128)(2,1)S(1)}, bf16[128,4,128]{2,0,1:T(8,128)(2,1)S(1)}, u32[]{:S(2)}, u32[]{:S(2)}) collective-permute-start(bf16[128,4,128]{2,0,1:T(8,128)(2,1)S(1)} %get-tuple-element.926), channel_id=1, source_target_pairs={{0,1},{1,2},{2,3},{3,4},{4,5},{5,6},{6,7},{7,0},{8,9},{9,10},{10,1... | collective-permute-start | bytes 393224 | tf_op jit(solution)/shard_map/while/body/eval_jaxpr/ppermute | solution.py:14
  170.4 14.1 %collective-permute-start.4 = (f32[128,4,128]{2,0,1:T(8,128)S(1)}, f32[128,4,128]{2,0,1:T(8,128)S(1)}, u32[]{:S(2)}, u32[]{:S(2)}) collective-permute-start(f32[128,4,128]{2,0,1:T(8,128)S(1)} %get-tuple-element.928), channel_id=1, source_target_pairs={{0,1},{1,2},{2,3},{3,4},{4,5},{5,6},{6,7},{7,0},{8,9},{9,10},{10,1... | collective-permute-start | bytes 786440 | tf_op jit(solution)/shard_map/while/body/eval_jaxpr/ppermute | solution.py:14
  170.5 19.7 %collective-permute-start.5 = (f32[128,4,128]{2,0,1:T(8,128)S(1)}, f32[128,4,128]{2,0,1:T(8,128)}, u32[]{:S(2)}, u32[]{:S(2)}) collective-permute-start(f32[128,4,128]{2,0,1:T(8,128)S(1)} %get-tuple-element.929), channel_id=1, source_target_pairs={{0,1},{1,2},{2,3},{3,4},{4,5},{5,6},{6,7},{7,0},{8,9},{9,10},{10,1... | collective-permute-start | bytes 786440 | tf_op jit(solution)/shard_map/while/body/eval_jaxpr/ppermute | solution.py:14
  170.6 19.5 %copy-start.10 = (bf16[128,4,128]{2,0,1:T(8,128)(2,1)S(1)}, bf16[128,4,128]{2,0,1:T(8,128)(2,1)}, u32[]{:S(2)}) copy-start(bf16[128,4,128]{2,0,1:T(8,128)(2,1)} %get-tuple-element.950) | copy-start | bytes 393220 | tf_op jit(solution)/shard_map/while
  191.4 11.0 %collective-permute-start.2 = (bf16[128,4,128]{2,0,1:T(8,128)(2,1)S(1)}, bf16[128,4,128]{2,0,1:T(8,128)(2,1)S(1)}, u32[]{:S(2)}, u32[]{:S(2)}) collective-permute-start(bf16[128,4,128]{2,0,1:T(8,128)(2,1)S(1)} %get-tuple-element.927), channel_id=1, source_target_pairs={{0,1},{1,2},{2,3},{3,4},{4,5},{5,6},{6,7},{7,0},{8,9},{9,10},{10,1... | collective-permute-start | bytes 393224 | tf_op jit(solution)/shard_map/while/body/eval_jaxpr/ppermute | solution.py:14
  191.5 10.6 %collective-permute-start.3 = (bf16[128,4,128]{2,0,1:T(8,128)(2,1)S(1)}, bf16[128,4,128]{2,0,1:T(8,128)(2,1)S(1)}, u32[]{:S(2)}, u32[]{:S(2)}) collective-permute-start(bf16[128,4,128]{2,0,1:T(8,128)(2,1)S(1)} %get-tuple-element.926), channel_id=1, source_target_pairs={{0,1},{1,2},{2,3},{3,4},{4,5},{5,6},{6,7},{7,0},{8,9},{9,10},{10,1... | collective-permute-start | bytes 393224 | tf_op jit(solution)/shard_map/while/body/eval_jaxpr/ppermute | solution.py:14
  193.1 14.7 %collective-permute-start.4 = (f32[128,4,128]{2,0,1:T(8,128)S(1)}, f32[128,4,128]{2,0,1:T(8,128)S(1)}, u32[]{:S(2)}, u32[]{:S(2)}) collective-permute-start(f32[128,4,128]{2,0,1:T(8,128)S(1)} %get-tuple-element.928), channel_id=1, source_target_pairs={{0,1},{1,2},{2,3},{3,4},{4,5},{5,6},{6,7},{7,0},{8,9},{9,10},{10,1... | collective-permute-start | bytes 786440 | tf_op jit(solution)/shard_map/while/body/eval_jaxpr/ppermute | solution.py:14
  193.2 20.3 %collective-permute-start.5 = (f32[128,4,128]{2,0,1:T(8,128)S(1)}, f32[128,4,128]{2,0,1:T(8,128)}, u32[]{:S(2)}, u32[]{:S(2)}) collective-permute-start(f32[128,4,128]{2,0,1:T(8,128)S(1)} %get-tuple-element.929), channel_id=1, source_target_pairs={{0,1},{1,2},{2,3},{3,4},{4,5},{5,6},{6,7},{7,0},{8,9},{9,10},{10,1... | collective-permute-start | bytes 786440 | tf_op jit(solution)/shard_map/while/body/eval_jaxpr/ppermute | solution.py:14
  193.3 20.2 %copy-start.10 = (bf16[128,4,128]{2,0,1:T(8,128)(2,1)S(1)}, bf16[128,4,128]{2,0,1:T(8,128)(2,1)}, u32[]{:S(2)}) copy-start(bf16[128,4,128]{2,0,1:T(8,128)(2,1)} %get-tuple-element.950) | copy-start | bytes 393220 | tf_op jit(solution)/shard_map/while
  214.7 10.0 %collective-permute-start.2 = (bf16[128,4,128]{2,0,1:T(8,128)(2,1)S(1)}, bf16[128,4,128]{2,0,1:T(8,128)(2,1)S(1)}, u32[]{:S(2)}, u32[]{:S(2)}) collective-permute-start(bf16[128,4,128]{2,0,1:T(8,128)(2,1)S(1)} %get-tuple-element.927), channel_id=1, source_target_pairs={{0,1},{1,2},{2,3},{3,4},{4,5},{5,6},{6,7},{7,0},{8,9},{9,10},{10,1... | collective-permute-start | bytes 393224 | tf_op jit(solution)/shard_map/while/body/eval_jaxpr/ppermute | solution.py:14
  214.8 9.7 %collective-permute-start.3 = (bf16[128,4,128]{2,0,1:T(8,128)(2,1)S(1)}, bf16[128,4,128]{2,0,1:T(8,128)(2,1)S(1)}, u32[]{:S(2)}, u32[]{:S(2)}) collective-permute-start(bf16[128,4,128]{2,0,1:T(8,128)(2,1)S(1)} %get-tuple-element.926), channel_id=1, source_target_pairs={{0,1},{1,2},{2,3},{3,4},{4,5},{5,6},{6,7},{7,0},{8,9},{9,10},{10,1... | collective-permute-start | bytes 393224 | tf_op jit(solution)/shard_map/while/body/eval_jaxpr/ppermute | solution.py:14
  214.9 15.3 %collective-permute-start.4 = (f32[128,4,128]{2,0,1:T(8,128)S(1)}, f32[128,4,128]{2,0,1:T(8,128)S(1)}, u32[]{:S(2)}, u32[]{:S(2)}) collective-permute-start(f32[128,4,128]{2,0,1:T(8,128)S(1)} %get-tuple-element.928), channel_id=1, source_target_pairs={{0,1},{1,2},{2,3},{3,4},{4,5},{5,6},{6,7},{7,0},{8,9},{9,10},{10,1... | collective-permute-start | bytes 786440 | tf_op jit(solution)/shard_map/while/body/eval_jaxpr/ppermute | solution.py:14
  215.0 20.9 %collective-permute-start.5 = (f32[128,4,128]{2,0,1:T(8,128)S(1)}, f32[128,4,128]{2,0,1:T(8,128)}, u32[]{:S(2)}, u32[]{:S(2)}) collective-permute-start(f32[128,4,128]{2,0,1:T(8,128)S(1)} %get-tuple-element.929), channel_id=1, source_target_pairs={{0,1},{1,2},{2,3},{3,4},{4,5},{5,6},{6,7},{7,0},{8,9},{9,10},{10,1... | collective-permute-start | bytes 786440 | tf_op jit(solution)/shard_map/while/body/eval_jaxpr/ppermute | solution.py:14
  215.1 20.8 %copy-start.10 = (bf16[128,4,128]{2,0,1:T(8,128)(2,1)S(1)}, bf16[128,4,128]{2,0,1:T(8,128)(2,1)}, u32[]{:S(2)}) copy-start(bf16[128,4,128]{2,0,1:T(8,128)(2,1)} %get-tuple-element.950) | copy-start | bytes 393220 | tf_op jit(solution)/shard_map/while
  237.8 9.4 %collective-permute-start.7 = (f32[128,4,128]{2,0,1:T(8,128)S(1)}, f32[128,4,128]{2,0,1:T(8,128)S(1)}, u32[]{:S(2)}, u32[]{:S(2)}) collective-permute-start(f32[128,4,128]{2,0,1:T(8,128)S(1)} %get-tuple-element.560), channel_id=1, source_target_pairs={{0,1},{1,2},{2,3},{3,4},{4,5},{5,6},{6,7},{7,0},{8,9},{9,10},{10,1... | collective-permute-start | bytes 786440 | tf_op jit(solution)/shard_map/ppermute | solution.py:14
  237.8 15.1 %collective-permute-start.6 = (f32[128,4,128]{2,0,1:T(8,128)}, f32[128,4,128]{2,0,1:T(8,128)S(1)}, u32[]{:S(2)}, u32[]{:S(2)}) collective-permute-start(f32[128,4,128]{2,0,1:T(8,128)} %copy-done.9), channel_id=1, source_target_pairs={{0,1},{1,2},{2,3},{3,4},{4,5},{5,6},{6,7},{7,0},{8,9},{9,10},{10,1... | collective-permute-start | bytes 786440 | tf_op jit(solution)/shard_map/ppermute | solution.py:14
  237.8 15.1 %copy-start.2 = (bf16[1,128,1024]{2,1,0:T(8,128)(2,1)S(1)}, bf16[1,128,1024]{2,1,0:T(8,128)(2,1)}, u32[]{:S(2)}) copy-start(bf16[1,128,1024]{2,1,0:T(8,128)(2,1)} %param.9) | copy-start | bytes 786436
  237.8 15.1 %copy-start.4 = (f32[128,2048]{1,0:T(8,128)S(1)}, f32[128,2048]{1,0:T(8,128)}, u32[]{:S(2)}) copy-start(f32[128,2048]{1,0:T(8,128)} %get-tuple-element.728) | copy-start | bytes 3145732
  264.5 560.4 %copy-start.5 = (f32[128,2048]{1,0:T(8,128)S(1)}, f32[128,2048]{1,0:T(8,128)}, u32[]{:S(2)}) copy-start(f32[128,2048]{1,0:T(8,128)} %get-tuple-element.728) | copy-start | bytes 3145732
  264.6 650.0 %all-gather.2.cloned.1.call-start = ((), (), s32[]{:S(2)}) async-start(), calls=%async_computation | async-start | bytes 5898240 | tf_op jit(solution)/shard_map/all_gather | solution.py:155
  918.3 7.4 slice-start
  918.3 8.7 copy-start.1
  (5 other events, 5.0 us)
Sparse Core Ops, SparseCore 0:
  264.7 442.0 all-reduce.3
  825.1 89.3 all-gather.1
where the time goes:
time: 935 us; the launch traced here: 934 us
  waiting for transfers between devices  682 us (73%)
  blocking collectives  117 us (13%)
  matrix products  38 us (4%)
  starting transfers between devices  36.7 us (4%)
  other arithmetic  24.3 us (3%)
  local copies, waits for them, and re-layouts  20 us (2%)
  between operations  15.1 us (2%)
    unnamed x3, waiting for transfers between devices  440 us
    ppermute x44, waiting for transfers between devices, passed_along(): lax.ppermute(array, axis, [(i, (i + by) % devices) for i in range(devices)])  157 us
    psum x1, blocking collectives, on_device(): shard_sum = lax.psum(shard_sum, 'dp')  117 us
    all_gather x1, waiting for transfers between devices, on_device(): lax.all_gather(shard_sum.astype(jnp.bfloat16), 'ctx', axis=0, tiled=True)  84.6 us
    ppermute x44, starting transfers between devices, passed_along(): lax.ppermute(array, axis, [(i, (i + by) % devices) for i in range(devices)])  36.6 us
  transfers between devices with their start and end apart: 46, of which 32 were waited for; matrix products, arithmetic and copies ran while one was open for 3% of the time, Pallas kernels for 0%

commit v1 on v0

v1 whole, which is shorter than its diff:
```python
import jax
import jax.numpy as jnp
from jax import lax
from jax.experimental import pallas as pl
from jax.experimental.pallas import tpu as pltpu
from jax.sharding import PartitionSpec as P

F32, BF16 = jnp.float32, jnp.bfloat16
MESH = pl.DeviceIdType.MESH
EPSILON = 1e-05
D = 1024
EVENTS = 1024
HD = 128
ROWS = 128
PAIR = 256
SCALE = HD ** (-0.5)
NT = (((1,), (1,)), ((), ()))


def dot(a, b):
    return jnp.dot(a, b, preferred_element_type=F32)


def dot_nt(a, b):
    return lax.dot_general(a, b, NT, preferred_element_type=F32)


def sigmoid(z):
    return 0.5 * jnp.tanh(0.5 * z) + 0.5


def device(x, yh, yl, z, c):
    return ((yl * 8 + z) * 2 + c, x * 2 + yh)


def remote(src, dst, send, recv, target):
    return pltpu.make_async_remote_copy(
        src_ref=src,
        dst_ref=dst,
        send_sem=send,
        recv_sem=recv,
        device_id=target,
        device_id_type=MESH,
    )


def kernel(
    hist, cot, lens, w_proj, w_out, d_hist, gs,
    xg, cg, xn, wp, wht, wo, lown, lsib, projt, spt, kr, vr, wm, sm, attnt, dgt, st, stx,
    gt, dat, dkt, dvt, dpt, dpr, pay, ybuf, zsend, zbuf, dn,
    wsem, osem, lsem, swsem, xsem, xrsem, fsem, frsem, csem, crsem, gsem, grsem, stsem, strsem,
    asem, arsem, asem0, ysem, yrsem, zsem, zrsem, g1s, g1r, g2s, g2r, g3s, g3r, g4s, g4r,
):
    dp, ctx = lax.axis_index("dp"), lax.axis_index("ctx")
    c, z, yl = lax.rem(dp, 2), lax.rem(dp // 2, 8), dp // 16
    x, yh = ctx // 2, lax.rem(ctx, 2)
    y = yh * 2 + yl
    sib = device(x, yh, yl, z, 1 - c)

    def x_mate(d):
        return device(lax.rem(x + d, 4), yh, yl, z, c)

    def y_mate(d):
        other = lax.rem(y + d, 4)
        return device(x, other // 2, lax.rem(other, 2), z, c)

    def z_mate(d):
        return device(x, yh, yl, lax.rem(z + d, 8), c)

    def x_from(d):
        return lax.rem(x + 4 - d, 4)

    def y_from(d):
        return lax.rem(y + 4 - d, 4)

    def z_from(d):
        return lax.rem(z + 8 - d, 8)

    get_w = pltpu.make_async_copy(w_proj, wp, wsem)
    get_w.start()
    get_o = pltpu.make_async_copy(w_out.at[pl.ds(pl.multiple_of(x * HD, HD), HD), :], wo, osem)
    get_o.start()

    barrier = pltpu.get_barrier_semaphore()
    group = [(i // 4, (i // 2) % 2, i % 2) for i in range(1, 16)]
    mates = [device(lax.rem(x + a, 4), lax.rem(yh + b, 2), yl, z, lax.rem(c + e, 2)) for a, b, e in group]
    mates += [z_mate(d) for d in range(1, 8)] + [y_mate(1), y_mate(3)]
    for mate in mates:
        pl.semaphore_signal(barrier, inc=1, device_id=mate, device_id_type=MESH)

    lane = lax.broadcasted_iota(jnp.int32, (8, 128), 1)
    first = jnp.broadcast_to(lens[0:1, 0:1], (8, 128))
    second = first + jnp.broadcast_to(lens[0:1, 1:2], (8, 128))
    lown[...] = jnp.where(lane == 0, first, jnp.where(lane == 1, second, 0))

    pl.semaphore_wait(barrier, len(mates))

    slot = pl.ds(pl.multiple_of((2 * x + c) * ROWS, ROWS), ROWS)
    over = pl.ds(pl.multiple_of((2 * x + 1 - c) * ROWS, ROWS), ROWS)
    here = c == yh
    swap = device(x, 1 - yh, yl, z, 1 - c)
    swap_x = remote(hist, xg.at[over, :], swsem.at[0], swsem.at[1], swap)
    swap_c = remote(cot, cg.at[over, :], swsem.at[2], swsem.at[3], swap)
    send_l = remote(lown, lsib, lsem.at[0], lsem.at[1], sib)
    send_l.start()

    @pl.when(here)
    def _():
        xg[slot, :] = hist[...]
        cg[slot, :] = cot[...]

    @pl.when(jnp.logical_not(here))
    def _():
        swap_x.start()
        swap_c.start()
        swap_x.wait_recv()

    def block_of(d, core):
        return pl.ds(pl.multiple_of((2 * x_from(d) + core) * ROWS, ROWS), ROWS)

    push_x = [remote(xg.at[slot, :], xg.at[slot, :], xsem.at[d], xrsem.at[d], x_mate(d)) for d in range(1, 4)]
    push_c = [remote(cg.at[slot, :], cg.at[slot, :], csem.at[d], crsem.at[d], x_mate(d)) for d in range(1, 4)]
    pass_x = [remote(xg.at[block_of(d, c), :], xg.at[block_of(d, c), :], fsem.at[d], frsem.at[d], sib) for d in range(4)]
    pass_c = [remote(cg.at[block_of(d, c), :], cg.at[block_of(d, c), :], gsem.at[d], grsem.at[d], sib) for d in range(4)]
    for copy in push_x:
        copy.start()
    pass_x[0].start()

    get_w.wait()
    for j in range(4):
        columns = pl.ds(pl.multiple_of(j * 512 + x * HD, HD), HD)
        wht[j * HD : (j + 1) * HD, :] = wp[:, columns].T

    def project(d):
        base = x_from(d) * PAIR

        @pl.loop(0, PAIR // 32)
        def _(i):
            rows = pl.ds(pl.multiple_of(base + i * 32, 32), 32)
            values = xg[rows, :].astype(F32)
            centred = values - jnp.mean(values, axis=-1, keepdims=True)
            variance = jnp.mean(centred * centred, axis=-1, keepdims=True)
            xn[rows, :] = (centred * lax.rsqrt(variance + EPSILON)).astype(BF16)

        rows = pl.ds(pl.multiple_of(base, PAIR), PAIR)
        normed = xn[rows, :]
        for j in range(4):
            pre = dot_nt(wht[j * HD : (j + 1) * HD, :], normed)
            s = sigmoid(pre)
            value = pre * s
            spt[j * HD : (j + 1) * HD, rows] = s + value * (1.0 - s)
            value = value.astype(BF16)
            projt[j * HD : (j + 1) * HD, rows] = value
            if j == 1:
                vr[rows, :] = value.T
            if j == 3:
                kr[rows, :] = value.T

    for d in (0, 1, 3, 2):
        if d:
            push_x[d - 1].wait_recv()
            pass_x[d].start()
        if d == 2:
            @pl.when(jnp.logical_not(here))
            def _():
                swap_c.wait_recv()

            for copy in push_c:
                copy.start()
            pass_c[0].start()
        pass_x[d].wait_recv()
        project(d)

    send_l.wait_recv()
    ends = jnp.where(here, lown[...], lsib[...])
    first, second = ends[0:1, 0:1], ends[0:1, 1:2]

    for pb in range(4):
        cols = slice(pb * PAIR, (pb + 1) * PAIR)
        q = projt[2 * HD : 3 * HD, cols]
        p_at = lax.broadcasted_iota(jnp.int32, (1, PAIR), 1) + pb * PAIR
        p_end = jnp.where(p_at < first, first, jnp.where(p_at < second, second, EVENTS))
        total = None
        for rb in range(pb, 4):
            rows = slice(rb * PAIR, (rb + 1) * PAIR)
            logits = dot(kr[rows, :], q) * SCALE
            s = sigmoid(logits)
            weight = logits * s
            slope = s + weight * (1.0 - s)
            r_at = lax.broadcasted_iota(jnp.int32, (PAIR, PAIR), 0) + rb * PAIR
            allowed = (r_at >= p_at) & (r_at < p_end)
            weight = jnp.where(allowed, weight, 0.0).astype(BF16)
            wm[rows, cols] = weight
            sm[rows, cols] = jnp.where(allowed, slope, 0.0)
            term = dot(projt[HD : 2 * HD, rows], weight)
            total = term if total is None else total + term
        attnt[:, cols] = total

    for d in (1, 3, 2):
        push_c[d - 1].wait_recv()
        pass_c[d].start()
    for d in range(4):
        pass_c[d].wait_recv()
    get_o.wait()

    st[4:8, :] = jnp.zeros((4, EVENTS), F32)
    for pb in range(4):
        cols = slice(pb * PAIR, (pb + 1) * PAIR)
        d_gated = dot_nt(wo[...], cg[cols, :])
        dgt[:, cols] = d_gated
        attn = attnt[:, cols]
        g = d_gated * projt[0:HD, cols].astype(F32)
        average = jnp.mean(attn, axis=0, keepdims=True)
        centred = attn - average
        st[0:1, cols] = average
        st[1:2, cols] = jnp.sum(centred * centred, axis=0, keepdims=True)
        st[2:3, cols] = jnp.sum(g, axis=0, keepdims=True)
        st[3:4, cols] = jnp.sum(g * centred, axis=0, keepdims=True)

    push_s = [remote(st, stx.at[d], stsem.at[d], strsem.at[d], x_mate(d)) for d in range(1, 4)]
    for copy in push_s:
        copy.start()
    for copy in push_s:
        copy.wait_recv()
    parts = [st[...]] + [stx[d] for d in range(1, 4)]
    average = (parts[0][0:1] + parts[1][0:1] + parts[2][0:1] + parts[3][0:1]) * 0.25
    spread = sum(p[1:2] + HD * (p[0:1] - average) ** 2 for p in parts) * (1.0 / 512)
    a_scale = lax.rsqrt(spread + EPSILON)
    g_mean = sum(p[2:3] for p in parts) * (1.0 / 512)
    ga_mean = a_scale * (sum(p[3:4] + (p[0:1] - average) * p[2:3] for p in parts) * (1.0 / 512))

    for pb in range(4):
        cols = slice(pb * PAIR, (pb + 1) * PAIR)
        u = projt[0:HD, cols].astype(F32)
        d_gated = dgt[:, cols]
        scale = a_scale[:, cols]
        a_norm = (attnt[:, cols] - average[:, cols]) * scale
        gt[:, cols] = (a_norm * u).astype(BF16)
        dpt[0, :, cols] = (d_gated * a_norm * spt[0:HD, cols]).astype(BF16)
        dat[:, cols] = (scale * (d_gated * u - g_mean[:, cols] - a_norm * ga_mean[:, cols])).astype(BF16)

    for pb in range(4):
        cols = slice(pb * PAIR, (pb + 1) * PAIR)
        q = projt[2 * HD : 3 * HD, cols]
        da = dat[:, cols]
        total = None
        for rb in range(pb, 4):
            rows = slice(rb * PAIR, (rb + 1) * PAIR)
            d_logits = (dot(vr[rows, :], da) * sm[rows, cols]).astype(BF16)
            term = dot(projt[3 * HD : 4 * HD, rows], d_logits)
            total = term if total is None else total + term
            d_key = dot_nt(q, d_logits)
            d_value = dot_nt(da, wm[rows, cols])
            if pb == 0:
                dkt[:, rows] = d_key
                dvt[:, rows] = d_value
            else:
                dkt[:, rows] += d_key
                dvt[:, rows] += d_value
        dpt[2, :, cols] = (total * SCALE * spt[2 * HD : 3 * HD, cols]).astype(BF16)
    dpt[1] = (dvt[...] * spt[HD : 2 * HD, :]).astype(BF16)
    dpt[3] = (dkt[...] * SCALE * spt[3 * HD : 4 * HD, :]).astype(BF16)

    mine = pl.ds(2 * c, 2)
    backs = []
    for dx in range(4):
        for dy in range(2):
            tx, ty = lax.rem(x + dx, 4), lax.rem(yh + dy, 2)
            lanes = pl.ds(pl.multiple_of((tx * 2 + ty) * ROWS, ROWS), ROWS)
            copy = remote(
                dpt.at[mine, :, lanes], dpr.at[mine, x], asem.at[dx * 2 + dy], arsem.at[dx * 2 + c], device(tx, ty, yl, z, yh)
            )
            if dx == 0 and dy == 0:
                @pl.when(jnp.logical_not(here))
                def _(copy=copy):
                    copy.start()

                @pl.when(here)
                def _(lanes=lanes):
                    pltpu.make_async_copy(dpt.at[mine, :, lanes], dpr.at[mine, x], asem0).start()
            else:
                copy.start()
            backs.append(copy)

    half = pl.ds(pl.multiple_of(c * 512, 512), 512)
    grad_o = dot(gt[...], cg[:, half]).astype(BF16)
    for j in range(4):
        pay[j, 512:640, :] = grad_o[:, j * HD : (j + 1) * HD]
    push_y = []
    for d in (1, 3, 2, 0):
        j = lax.rem(y + d, 4)
        pay[j, 0:512, :] = dot(dpt[j], xn[:, half]).T.astype(BF16)
        if d:
            copy = remote(pay.at[j], ybuf.at[d], ysem.at[d], yrsem.at[d], y_mate(d))
            copy.start()
            push_y.append(copy)
    for copy in push_y:
        copy.wait_recv()
    zsend[...] = (
        pay[y].astype(F32) + ybuf[1].astype(F32) + ybuf[2].astype(F32) + ybuf[3].astype(F32)
    ).astype(BF16)
    push_z = []
    for d in (1, 7, 2, 6, 3, 5, 4):
        rows = pl.ds(pl.multiple_of(lax.rem(z + d, 8) * 80, 16), 80)
        copy = remote(zsend.at[rows, :], zbuf.at[d], zsem.at[d], zrsem.at[d], z_mate(d))
        copy.start()
        push_z.append(copy)
    for copy in push_z:
        copy.wait_recv()
    total = zsend[pl.ds(pl.multiple_of(z * 80, 16), 80), :].astype(F32)
    for d in range(1, 8):
        total = total + zbuf[d].astype(F32)
    gs[c, x, y, z] = total.astype(BF16)

    stage1 = []
    for d in range(1, 8):
        ref = gs.at[c, x, y, z, 0:64]
        stage1.append(remote(ref, ref, g1s.at[d], g1r.at[d], z_mate(d)))
    for d in range(1, 4):
        ref = gs.at[c, x, y, z, 64:80]
        stage1.append(remote(ref, ref, g1s.at[7 + d], g1r.at[7 + d], y_mate(d)))
    for copy in stage1:
        copy.start()

    for dx in range(4):
        for core in range(2):
            arrived = remote(
                dpr.at[pl.ds(2 * core, 2), x_from(dx)], dpr.at[pl.ds(2 * core, 2), x_from(dx)], asem.at[0], arsem.at[dx * 2 + core], sib
            )
            if dx == 0:
                local = here & (c == core)

                @pl.when(jnp.logical_not(local))
                def _(arrived=arrived):
                    arrived.wait_recv()

                @pl.when(local)
                def _(core=core):
                    ref = dpr.at[pl.ds(2 * core, 2), x]
                    pltpu.make_async_copy(ref, ref, asem0).wait()
            else:
                arrived.wait_recv()

    for copy in stage1:
        copy.wait_recv()
    stage2 = []
    for d in range(1, 4):
        ref = gs.at[c, x, y, :, 0:32]
        stage2.append(remote(ref, ref, g2s.at[d], g2r.at[d], y_mate(d)))
    for d in range(1, 4):
        ref = gs.at[c, x, y, :, 32:64]
        stage2.append(remote(ref, ref, g2s.at[3 + d], g2r.at[3 + d], x_mate(d)))
    for d in range(1, 4):
        ref = gs.at[c, x, :, z, 64:80]
        stage2.append(remote(ref, ref, g2s.at[6 + d], g2r.at[6 + d], x_mate(d)))
    for copy in stage2:
        copy.start()

    columns = dpr[...].reshape(2048, ROWS)
    for i in range(4):
        part = dot(wp[i * 256 : (i + 1) * 256, :], columns)
        dn[:, i * 256 : (i + 1) * 256] = part.T

    for copy in stage2:
        copy.wait_recv()
    stage3, stage4 = [], []

    def to_sibling(i, ref):
        copy = remote(ref, ref, g4s.at[i], g4r.at[i], sib)
        copy.start()
        stage4.append(copy)

    for d in range(1, 4):
        ref = gs.at[c, x, :, :, 0:32]
        stage3.append((remote(ref, ref, g3s.at[d], g3r.at[d], x_mate(d)), gs.at[c, x_from(d), :, :, 0:32]))
        ref = gs.at[c, :, y, :, 32:64]
        stage3.append((remote(ref, ref, g3s.at[3 + d], g3r.at[3 + d], y_mate(d)), gs.at[c, :, y_from(d), :, 32:64]))
    for d in (1, 7, 2, 6, 3, 5, 4):
        ref = gs.at[c, :, :, z, 64:80]
        stage3.append((remote(ref, ref, g3s.at[6 + d], g3r.at[6 + d], z_mate(d)), gs.at[c, :, :, z_from(d), 64:80]))
    for copy, _ in stage3:
        copy.start()
    to_sibling(0, gs.at[c, x, :, :, 0:32])
    to_sibling(1, gs.at[c, :, y, :, 32:64])
    to_sibling(2, gs.at[c, :, :, z, 64:80])

    @pl.loop(0, ROWS // 32)
    def _(i):
        rows = pl.ds(pl.multiple_of(i * 32, 32), 32)
        values = hist[rows, :].astype(F32)
        centred = values - jnp.mean(values, axis=-1, keepdims=True)
        variance = jnp.mean(centred * centred, axis=-1, keepdims=True)
        scale = lax.rsqrt(variance + EPSILON)
        normed = centred * scale
        grad = dn[rows, :]
        one = jnp.mean(grad, axis=-1, keepdims=True)
        two = jnp.mean(grad * normed, axis=-1, keepdims=True)
        d_hist[rows, :] = (cot[rows, :].astype(F32) + scale * (grad - one - normed * two)).astype(BF16)

    for i, (copy, ref) in enumerate(stage3):
        copy.wait_recv()
        to_sibling(3 + i, ref)
    for copy in stage4:
        copy.wait_recv()

    send_l.wait_send()

    @pl.when(jnp.logical_not(here))
    def _():
        swap_x.wait_send()
        swap_c.wait_send()
        backs[0].wait_send()

    sent = push_x + push_c + pass_x + pass_c + push_s + backs[1:] + push_y + push_z + stage1 + stage2
    for copy in sent + [copy for copy, _ in stage3] + stage4:
        copy.wait_send()


def on_device(history, cotangent, lengths, w_proj, w_out):
    vmem, dma = pltpu.VMEM, pltpu.SemaphoreType.DMA
    whole = pl.BlockSpec(memory_space=vmem)
    anywhere = pl.BlockSpec(memory_space=pl.ANY)
    scratch = [
        vmem((EVENTS, D), BF16),
        vmem((EVENTS, D), BF16),
        vmem((EVENTS, D), BF16),
        vmem((D, 2048), BF16),
        vmem((512, D), BF16),
        vmem((HD, D), BF16),
        vmem((8, 128), jnp.int32),
        vmem((8, 128), jnp.int32),
        vmem((512, EVENTS), BF16),
        vmem((512, EVENTS), F32),
        vmem((EVENTS, HD), BF16),
        vmem((EVENTS, HD), BF16),
        vmem((EVENTS, EVENTS), BF16),
        vmem((EVENTS, EVENTS), F32),
        vmem((HD, EVENTS), F32),
        vmem((HD, EVENTS), F32),
        vmem((8, EVENTS), F32),
        vmem((4, 8, EVENTS), F32),
        vmem((HD, EVENTS), BF16),
        vmem((HD, EVENTS), BF16),
        vmem((HD, EVENTS), F32),
        vmem((HD, EVENTS), F32),
        vmem((4, HD, EVENTS), BF16),
        vmem((4, 4, HD, ROWS), BF16),
        vmem((4, 640, HD), BF16),
        vmem((4, 640, HD), BF16),
        vmem((640, HD), BF16),
        vmem((8, 80, HD), BF16),
        vmem((ROWS, D), F32),
        dma, dma, dma((2,)), dma((4,)),
        dma((4,)), dma((4,)), dma((4,)), dma((4,)), dma((4,)), dma((4,)), dma((4,)), dma((4,)), dma((4,)), dma((4,)),
        dma((8,)), dma((8,)), dma, dma((4,)), dma((4,)), dma((8,)), dma((8,)),
        dma((11,)), dma((11,)), dma((10,)), dma((10,)), dma((14,)), dma((14,)), dma((16,)), dma((16,)),
    ]
    d_rows, sheets = pl.pallas_call(
        kernel,
        out_shape=(
            jax.ShapeDtypeStruct((ROWS, D), BF16),
            jax.ShapeDtypeStruct((2, 4, 4, 8, 80, HD), BF16),
        ),
        in_specs=[whole, whole, whole, anywhere, anywhere],
        out_specs=(whole, whole),
        scratch_shapes=scratch,
        compiler_params=pltpu.CompilerParams(
            collective_id=0, has_side_effects=True, vmem_limit_bytes=56 * 2**20
        ),
        name="layer",
    )(history[0], cotangent[0], lengths, w_proj, w_out)
    sheets = sheets.reshape(2, 4, 4, 640, HD)
    grad_p = sheets[:, :, :, :512].transpose(0, 3, 2, 1, 4).reshape(1024, 2048)
    grad_o = sheets[:, :, :, 512:].transpose(1, 3, 0, 2, 4).reshape(512, 1024)
    return d_rows[None], grad_p, grad_o


def solution(mesh):
    in_specs = (P("dp", "ctx", None), P("dp", "ctx", None), P("dp", None), P(), P())
    out_specs = (P("dp", "ctx", None), P(), P())
    return jax.shard_map(
        on_device, mesh=mesh, in_specs=in_specs, out_specs=out_specs, check_vma=False
    )
```

time: 935 us -> 127 us (0.14)
  waiting for transfers between devices: 682 us -> 0 us
  blocking collectives: 117 us -> 0 us
  Pallas kernels: 0 us -> 106 us
  matrix products: 38 us -> 0 us
  starting transfers between devices: 36.7 us -> 0 us
  other arithmetic: 24.3 us -> 0 us
  between operations: 15.1 us -> 0.66 us
    unnamed x3 -> x0, waiting for transfers between devices: 440 us -> none
    ppermute x44 -> x0, waiting for transfers between devices: 157 us -> none  [passed_along(): lax.ppermute(array, axis, [(i, (i + by) % devices) for i in range(devices)])]
    psum x1 -> x0, blocking collectives: 117 us -> none  [on_device(): shard_sum = lax.psum(shard_sum, 'dp')]
    pallas_call x0 -> x1, Pallas kernels: none -> 106 us  [on_device(): pl.pallas_call(kernel, out_shape=(jax.ShapeDtypeStruct((ROWS, D), BF16),...]
    all_gather x1 -> x0, waiting for transfers between devices: 84.6 us -> none  [on_device(): lax.all_gather(shard_sum.astype(jnp.bfloat16), 'ctx', axis=0, tiled=True)]
    dot_general x53 -> x0, matrix products: 38 us -> none  [the longest x8 9.75 us: backward_block(): jnp.einsum('hqk,qhd->khd', weights, d_heads, preferred_element_type=jnp.f...]
    ppermute x44 -> x0, starting transfers between devices: 36.6 us -> none  [passed_along(): lax.ppermute(array, axis, [(i, (i + by) % devices) for i in range(devices)])]
    reduce_sum x19 -> x0, other arithmetic: 12.7 us -> none  [the longest x15 10.1 us: segment_of(): jnp.sum((positions[:, None] >= history_ends[None, :]).astype(jnp.int32),...]
  transfers between devices with their start and end apart: 46 -> 0, of which waited for: 32 -> 0; matrix products, arithmetic and copies ran while one was open for 3% -> 0% of each run, Pallas kernels for 0% -> 0%
where the time goes in v1:
time: 127 us
  Pallas kernels  106 us (83%)
  local copies, waits for them, and re-layouts  19.8 us (16%)
    pallas_call x1, Pallas kernels, on_device(): pl.pallas_call(kernel, out_shape=(jax.ShapeDtypeStruct((ROWS, D), BF16),...  106 us
    reshape x1, local copies, waits for them, and re-layouts, on_device(): grad_p = sheets[:, :, :, :512].transpose(0, 3, 2, 1, 4).reshape(1024, 2048)  7.78 us
    transpose x2, local copies, waits for them, and re-layouts, on_device(): grad_p = sheets[:, :, :, :512].transpose(0, 3, 2, 1, 4).reshape(1024, 2048)  7.65 us

profile of v1, /device:TPU:1, one launch (start us, length us, event | category | flops | bytes accessed | tf_op | source)
XLA Modules:
  0.0 126.8 jit_solution(6508757059506647423)
XLA Ops:
  0.6 106.3 %layer.1 = (bf16[128,1024]{1,0:T(8,128)(2,1)}, bf16[2,4,4,8,80,128]{5,4,3,2,1,0:T(8,128)(2,1)}) custom-call(bf16[128,1024]{1,0:T(8,128)(2,1)} %bitcast.10, bf16[128,1024]{1,0:T(8,128)(2,1)} %bitcast.11, s32[1,3]{1,0:T(1,128)} %lens.1, bf16[1024,2048]{1,0:T(8,128)(2,1)} %w_proj.1, bf16[512,1024]{1,0:T(8,128)(2,1)} %w_out.1), custom_call_target="tpu_custom_call" | custom-call | tf_op jit(solution)/shard_map/layer/pallas_call | solution.py:458
  107.0 1.3 %slice_bitcast_fusion.1 = bf16[4,128,2,4,128]{4,1,3,0,2:T(8,128)(2,1)S(1)} fusion(bf16[2,4,4,640,128]{4,3,2,1,0:T(8,128)(2,1)} %bitcast.8), kind=kLoop, calls=%fused_computation.1 | loop fusion | bytes 2097152 | tf_op jit(solution)/shard_map/transpose | solution.py:474
  108.3 2.5 %slice_bitcast_fusion = bf16[2,512,4,4,128]{4,1,2,3,0:T(8,128)(2,1)S(1)} fusion(bf16[2,4,4,640,128]{4,3,2,1,0:T(8,128)(2,1)} %bitcast.9), kind=kLoop, calls=%fused_computation | loop fusion | bytes 8388608 | tf_op jit(solution)/shard_map/transpose | solution.py:473
  110.8 5.2 %copy.8 = bf16[2,512,4,4,128]{4,3,2,1,0:T(4,128)(2,1)} copy(bf16[2,512,4,4,128]{4,1,2,3,0:T(8,128)(2,1)S(1)} %slice_bitcast_fusion) | data formatting | bytes 8388608 | tf_op jit(solution)/shard_map/transpose | solution.py:473
  116.0 7.8 %reshape.16 = bf16[1024,2048]{1,0:T(8,128)(2,1)} reshape(bf16[2,512,4,4,128]{4,3,2,1,0:T(4,128)(2,1)} %copy.8) | data formatting | bytes 8388608 | tf_op jit(solution)/shard_map/reshape | solution.py:473
  123.7 0.0 copy-start
  123.7 0.8 copy.9
  124.6 1.5 %reshape.17 = bf16[512,1024]{1,0:T(8,128)(2,1)} reshape(bf16[4,128,2,4,128]{4,3,2,1,0:T(4,128)(2,1)S(1)} %copy.9) | data formatting | bytes 2097152 | tf_op jit(solution)/shard_map/reshape | solution.py:474
  126.1 0.0 copy-done
  126.1 0.7 copy.11
Async XLA Ops:
  123.7 2.4 %copy-start = (bf16[128,1024]{1,0:T(8,128)(2,1)S(1)}, bf16[128,1024]{1,0:T(8,128)(2,1)}, u32[]{:S(2)}) copy-start(bf16[128,1024]{1,0:T(8,128)(2,1)} %get-tuple-element.5) | copy-start | bytes 786436

commit v2 on v1

v2 whole, which is shorter than its diff:
```python
import jax
import jax.numpy as jnp
from jax import lax
from jax.experimental import pallas as pl
from jax.experimental.pallas import tpu as pltpu
from jax.sharding import PartitionSpec as P

F32, BF16 = jnp.float32, jnp.bfloat16
MESH = pl.DeviceIdType.MESH
EPSILON = 1e-05
D = 1024
EVENTS = 1024
HD = 128
ROWS = 128
PAIR = 256
SCALE = HD ** (-0.5)
NT = (((1,), (1,)), ((), ()))


def dot(a, b):
    return jnp.dot(a, b, preferred_element_type=F32)


def dot_nt(a, b):
    return lax.dot_general(a, b, NT, preferred_element_type=F32)


def sigmoid(z):
    return 0.5 * jnp.tanh(0.5 * z) + 0.5


def device(x, yh, yl, z, c):
    return ((yl * 8 + z) * 2 + c, x * 2 + yh)


def remote(src, dst, send, recv, target):
    return pltpu.make_async_remote_copy(
        src_ref=src,
        dst_ref=dst,
        send_sem=send,
        recv_sem=recv,
        device_id=target,
        device_id_type=MESH,
    )


class Flight:
    def __init__(self):
        self.unsent, self.unreceived = [], []

    @staticmethod
    def do(action, when):
        if when is None:
            action()
        else:
            pl.when(when)(action)

    def start(self, copy, when=None, mirrored=True):
        self.do(copy.start, when)
        self.unsent.append((copy.wait_send, when))
        if mirrored:
            self.expect(copy, copy.wait_recv, when)

    def start_local(self, copy, when=None):
        self.do(copy.start, when)
        self.expect(copy, copy.wait, when)

    def expect(self, copy, wait, when=None):
        self.unreceived.append((copy, wait, when))

    def receive(self, copy):
        (entry,) = [e for e in self.unreceived if e[0] is copy]
        self.unreceived = [e for e in self.unreceived if e[0] is not copy]
        self.do(entry[1], entry[2])

    def land(self):
        for entry in list(self.unreceived):
            self.receive(entry[0])
        for wait, when in self.unsent:
            self.do(wait, when)


def kernel(
    hist_in, cot_in, lens, w_proj, w_out, d_hist, gp, go,
    hist, cot, xg, cg, xn, wp, wht, wo, lown, lsib, projt, spt, kr, vr, wm, sm, attnt, dgt, st, stx,
    gt, dat, dkt, dvt, dpt, dpr, pay, ybuf, zsend, zbuf, piece_p, piece_o, dn,
    known, insem, wsem, osem, lsem, swsem, xsem, xrsem, fsem, frsem, csem, crsem, gsem, grsem, stsem, strsem,
    asem, arsem, asem0, ysem, yrsem, zsem, zrsem, g0, g1s, g1r, g2s, g2r, g3s, g3r, g4s, g4r,
):
    dp, ctx = lax.axis_index("dp"), lax.axis_index("ctx")
    c, z, yl = lax.rem(dp, 2), lax.rem(dp // 2, 8), dp // 16
    x, yh = ctx // 2, lax.rem(ctx, 2)
    y = yh * 2 + yl
    sib = device(x, yh, yl, z, 1 - c)

    def x_mate(d):
        return device(lax.rem(x + d, 4), yh, yl, z, c)

    def y_mate(d):
        other = lax.rem(y + d, 4)
        return device(x, other // 2, lax.rem(other, 2), z, c)

    def z_mate(d):
        return device(x, yh, yl, lax.rem(z + d, 8), c)

    def x_from(d):
        return lax.rem(x + 4 - d, 4)

    def y_from(d):
        return lax.rem(y + 4 - d, 4)

    def z_from(d):
        return lax.rem(z + 8 - d, 8)

    here = c == yh
    away = jnp.logical_not(here)
    flight = Flight()

    get_w = pltpu.make_async_copy(w_proj, wp, wsem)
    get_o = pltpu.make_async_copy(w_out.at[pl.ds(pl.multiple_of(x * HD, HD), HD), :], wo, osem)
    get_x = pltpu.make_async_copy(hist_in, hist, insem.at[0])
    get_c = pltpu.make_async_copy(cot_in, cot, insem.at[1])
    flight.start_local(get_x)
    flight.start_local(get_c)
    flight.start_local(get_w)
    flight.start_local(get_o)

    barrier = pltpu.get_barrier_semaphore()
    swap = device(x, 1 - yh, yl, z, 1 - c)
    near = [sib, swap] + [x_mate(d) for d in range(1, 4)] + [y_mate(d) for d in range(1, 4)] + [z_mate(1), z_mate(7)]
    for mate in near:
        pl.semaphore_signal(barrier, inc=1, device_id=mate, device_id_type=MESH)

    def tell(level):
        for mate in (sib, y_mate(2), z_mate(1), z_mate(7)):
            pl.semaphore_signal(known.at[level], inc=1, device_id=mate, device_id_type=MESH)

    def hear(level):
        pl.semaphore_wait(known.at[level], 4)

    lane = lax.broadcasted_iota(jnp.int32, (8, 128), 1)
    first = jnp.broadcast_to(lens[0:1, 0:1], (8, 128))
    second = first + jnp.broadcast_to(lens[0:1, 1:2], (8, 128))
    lown[...] = jnp.where(lane == 0, first, jnp.where(lane == 1, second, 0))

    pl.semaphore_wait(barrier, len(near))
    tell(0)

    slot = pl.ds(pl.multiple_of((2 * x + c) * ROWS, ROWS), ROWS)
    over = pl.ds(pl.multiple_of((2 * x + 1 - c) * ROWS, ROWS), ROWS)
    swap_x = remote(hist, xg.at[over, :], swsem.at[0], swsem.at[1], swap)
    swap_c = remote(cot, cg.at[over, :], swsem.at[2], swsem.at[3], swap)
    flight.receive(get_x)
    flight.start(swap_x, away)
    send_l = remote(lown, lsib, lsem.at[0], lsem.at[1], sib)
    flight.start(send_l)

    @pl.when(here)
    def _():
        xg[slot, :] = hist[...]

    flight.receive(swap_x)
    flight.receive(get_c)
    flight.start(swap_c, away)

    def block_of(d, core):
        return pl.ds(pl.multiple_of((2 * x_from(d) + core) * ROWS, ROWS), ROWS)

    push_x = [remote(xg.at[slot, :], xg.at[slot, :], xsem.at[d], xrsem.at[d], x_mate(d)) for d in range(1, 4)]
    push_c = [remote(cg.at[slot, :], cg.at[slot, :], csem.at[d], crsem.at[d], x_mate(d)) for d in range(1, 4)]
    pass_x = [remote(xg.at[block_of(d, c), :], xg.at[block_of(d, c), :], fsem.at[d], frsem.at[d], sib) for d in range(4)]
    pass_c = [remote(cg.at[block_of(d, c), :], cg.at[block_of(d, c), :], gsem.at[d], grsem.at[d], sib) for d in range(4)]
    for copy in push_x:
        flight.start(copy)
    flight.start(pass_x[0])

    flight.receive(get_w)
    for j in range(4):
        columns = pl.ds(pl.multiple_of(j * 512 + x * HD, HD), HD)
        wht[j * HD : (j + 1) * HD, :] = wp[:, columns].T

    def project(d):
        base = x_from(d) * PAIR

        @pl.loop(0, PAIR // 16, unroll=4)
        def _(i):
            rows = pl.ds(pl.multiple_of(base + i * 16, 16), 16)
            values = xg[rows, :].astype(F32)
            centred = values - jnp.mean(values, axis=-1, keepdims=True)
            variance = jnp.mean(centred * centred, axis=-1, keepdims=True)
            xn[rows, :] = (centred * lax.rsqrt(variance + EPSILON)).astype(BF16)

        rows = pl.ds(pl.multiple_of(base, PAIR), PAIR)
        normed = xn[rows, :]
        pres = dot_nt(wht[...], normed)
        for j in range(4):
            pre = pres[j * HD : (j + 1) * HD]
            s = sigmoid(pre)
            value = pre * s
            spt[j * HD : (j + 1) * HD, rows] = s + value * (1.0 - s)
            value = value.astype(BF16)
            projt[j * HD : (j + 1) * HD, rows] = value
            if j == 1:
                vr[rows, :] = value.T
            if j == 3:
                kr[rows, :] = value.T

    flight.receive(pass_x[0])
    project(0)
    hear(0)
    tell(1)
    for d in (1, 3):
        flight.receive(push_x[d - 1])
        flight.start(pass_x[d])
    flight.receive(swap_c)

    @pl.when(here)
    def _():
        cg[slot, :] = cot[...]

    for copy in push_c:
        flight.start(copy)
    flight.start(pass_c[0])
    for d in (1, 3):
        flight.receive(pass_x[d])
        project(d)
    hear(1)
    tell(2)
    flight.receive(push_x[1])
    flight.start(pass_x[2])
    flight.receive(pass_x[2])
    project(2)

    hear(2)
    flight.receive(send_l)
    ends = jnp.where(here, lown[...], lsib[...])
    first, second = ends[0:1, 0:1], ends[0:1, 1:2]

    for pb in range(4):
        cols = slice(pb * PAIR, (pb + 1) * PAIR)
        q = projt[2 * HD : 3 * HD, cols]
        p_at = lax.broadcasted_iota(jnp.int32, (1, PAIR), 1) + pb * PAIR
        p_end = jnp.where(p_at < first, first, jnp.where(p_at < second, second, EVENTS))
        total = None
        for rb in range(pb, 4):
            rows = slice(rb * PAIR, (rb + 1) * PAIR)
            logits = dot(kr[rows, :], q) * SCALE
            s = sigmoid(logits)
            weight = logits * s
            slope = s + weight * (1.0 - s)
            r_at = lax.broadcasted_iota(jnp.int32, (PAIR, PAIR), 0) + rb * PAIR
            allowed = (r_at >= p_at) & (r_at < p_end)
            weight = jnp.where(allowed, weight, 0.0).astype(BF16)
            wm[rows, cols] = weight
            sm[rows, cols] = jnp.where(allowed, slope, 0.0)
            term = dot(projt[HD : 2 * HD, rows], weight)
            total = term if total is None else total + term
        attnt[:, cols] = total

    for d in (1, 3, 2):
        flight.receive(push_c[d - 1])
        flight.start(pass_c[d])
    for d in range(4):
        flight.receive(pass_c[d])
    flight.receive(get_o)

    st[4:8, :] = jnp.zeros((4, EVENTS), F32)
    for pb in range(4):
        cols = slice(pb * PAIR, (pb + 1) * PAIR)
        d_gated = dot_nt(wo[...], cg[cols, :])
        dgt[:, cols] = d_gated
        attn = attnt[:, cols]
        g = d_gated * projt[0:HD, cols].astype(F32)
        average = jnp.mean(attn, axis=0, keepdims=True)
        centred = attn - average
        st[0:1, cols] = average
        st[1:2, cols] = jnp.sum(centred * centred, axis=0, keepdims=True)
        st[2:3, cols] = jnp.sum(g, axis=0, keepdims=True)
        st[3:4, cols] = jnp.sum(g * centred, axis=0, keepdims=True)

    push_s = [remote(st, stx.at[d], stsem.at[d], strsem.at[d], x_mate(d)) for d in range(1, 4)]
    for copy in push_s:
        flight.start(copy)
    for copy in push_s:
        flight.receive(copy)
    parts = [st[...]] + [stx[d] for d in range(1, 4)]
    average = (parts[0][0:1] + parts[1][0:1] + parts[2][0:1] + parts[3][0:1]) * 0.25
    spread = sum(p[1:2] + HD * (p[0:1] - average) ** 2 for p in parts) * (1.0 / 512)
    a_scale = lax.rsqrt(spread + EPSILON)
    g_mean = sum(p[2:3] for p in parts) * (1.0 / 512)
    ga_mean = a_scale * (sum(p[3:4] + (p[0:1] - average) * p[2:3] for p in parts) * (1.0 / 512))

    for pb in range(4):
        cols = slice(pb * PAIR, (pb + 1) * PAIR)
        u = projt[0:HD, cols].astype(F32)
        d_gated = dgt[:, cols]
        scale = a_scale[:, cols]
        a_norm = (attnt[:, cols] - average[:, cols]) * scale
        gt[:, cols] = (a_norm * u).astype(BF16)
        dpt[0, :, cols] = (d_gated * a_norm * spt[0:HD, cols]).astype(BF16)
        dat[:, cols] = (scale * (d_gated * u - g_mean[:, cols] - a_norm * ga_mean[:, cols])).astype(BF16)

    for pb in range(4):
        cols = slice(pb * PAIR, (pb + 1) * PAIR)
        q = projt[2 * HD : 3 * HD, cols]
        da = dat[:, cols]
        total = None
        for rb in range(pb, 4):
            rows = slice(rb * PAIR, (rb + 1) * PAIR)
            d_logits = (dot(vr[rows, :], da) * sm[rows, cols]).astype(BF16)
            term = dot(projt[3 * HD : 4 * HD, rows], d_logits)
            total = term if total is None else total + term
            d_key = dot_nt(q, d_logits)
            d_value = dot_nt(da, wm[rows, cols])
            if pb == 0:
                dkt[:, rows] = d_key
                dvt[:, rows] = d_value
            else:
                dkt[:, rows] += d_key
                dvt[:, rows] += d_value
        dpt[2, :, cols] = (total * SCALE * spt[2 * HD : 3 * HD, cols]).astype(BF16)
    dpt[1] = (dvt[...] * spt[HD : 2 * HD, :]).astype(BF16)
    dpt[3] = (dkt[...] * SCALE * spt[3 * HD : 4 * HD, :]).astype(BF16)

    half = pl.ds(pl.multiple_of(c * 512, 512), 512)
    grad_o = dot(gt[...], cg[:, half]).astype(BF16)
    for j in range(4):
        pay[j, :, 64:80, :] = grad_o[:, j * HD : (j + 1) * HD].reshape(8, 16, HD)
    push_y = []
    for d in (1, 3, 2, 0):
        j = lax.rem(y + d, 4)
        pay[j, :, 0:64, :] = dot(dpt[j], xn[:, half]).T.astype(BF16).reshape(8, 64, HD)
        if d:
            copy = remote(pay.at[j], ybuf.at[d], ysem.at[d], yrsem.at[d], y_mate(d))
            flight.start(copy)
            push_y.append(copy)
    for copy in push_y:
        flight.receive(copy)
    zsend[...] = (
        pay[y].astype(F32) + ybuf[1].astype(F32) + ybuf[2].astype(F32) + ybuf[3].astype(F32)
    ).astype(BF16)
    push_z = []
    for d in (1, 7, 2, 6, 3, 5, 4):
        copy = remote(zsend.at[lax.rem(z + d, 8)], zbuf.at[d], zsem.at[d], zrsem.at[d], z_mate(d))
        flight.start(copy)
        push_z.append(copy)
    mine = pl.ds(2 * c, 2)
    for dx in range(4):
        for dy in range(2):
            tx, ty = lax.rem(x + dx, 4), lax.rem(yh + dy, 2)
            lanes = pl.ds(pl.multiple_of((tx * 2 + ty) * ROWS, ROWS), ROWS)
            source, place = dpt.at[mine, :, lanes], dpr.at[mine, x]
            copy = remote(source, place, asem.at[dx * 2 + dy], arsem.at[dx * 2 + c], device(tx, ty, yl, z, yh))
            if dx or dy:
                flight.start(copy, mirrored=False)
            else:
                flight.start(copy, away, mirrored=False)
                keep = pltpu.make_async_copy(source, place, asem0)
                flight.start_local(keep, here)
    arrivals = [keep]
    for dx in range(4):
        for core in range(2):
            place = dpr.at[pl.ds(2 * core, 2), x_from(dx)]
            copy = remote(place, place, asem.at[0], arsem.at[dx * 2 + core], sib)
            flight.expect(copy, copy.wait_recv, None if dx else jnp.logical_not(here & (c == core)))
            arrivals.append(copy)

    for copy in push_z:
        flight.receive(copy)
    total = zsend[z].astype(F32)
    for d in range(1, 8):
        total = total + zbuf[d].astype(F32)
    total = total.astype(BF16)
    piece_p[...] = total[0:64].reshape(2, 32, HD)
    piece_o[...] = total[64:80]

    def kind_at(j, head):
        return pl.ds(pl.multiple_of(j * 512 + head * HD, HD), HD)

    own_p = gp.at[c, z, :, :, kind_at(y, x)]
    own_o = go.at[x, z, :, pl.ds(pl.multiple_of(c * 512 + y * HD, HD), HD)]
    keep_p = pltpu.make_async_copy(piece_p, own_p, g0.at[0])
    keep_o = pltpu.make_async_copy(piece_o, own_o, g0.at[1])
    stage1 = [keep_p, keep_o]
    for d in (1, 7, 2, 6, 3, 5, 4):
        stage1.append(remote(piece_p, own_p, g1s.at[d], g1r.at[d], z_mate(d)))
    for d in range(1, 4):
        stage1.append(remote(piece_o, own_o, g1s.at[7 + d], g1r.at[7 + d], y_mate(d)))
    flight.start_local(keep_p)
    flight.start_local(keep_o)
    for copy in stage1[2:]:
        flight.start(copy)

    stage4 = []

    def to_sibling(ref):
        i = len(stage4)
        copy = remote(ref, ref, g4s.at[i], g4r.at[i], sib)
        flight.start(copy)
        stage4.append(copy)

    def part_a(kind, head):
        return gp.at[c, :, 0, :, kind_at(kind, head)]

    def part_b(kind, head):
        return gp.at[c, :, 1, :, kind_at(kind, head)]

    def out_row(copies):
        for copy in copies:
            flight.start(copy)
        return copies

    flight.receive(keep_o)
    for copy in stage1[9:]:
        flight.receive(copy)
    ref = go.at[x, z, :, half]
    second_c = out_row([remote(ref, ref, g2s.at[6 + d], g2r.at[6 + d], x_mate(d)) for d in range(1, 4)])

    def third_a(dj):
        ref = part_a(y_from(dj), x)
        to_sibling(ref)
        return out_row([remote(ref, ref, g3s.at[dj * 4 + d], g3r.at[dj * 4 + d], x_mate(d)) for d in (1, 3, 2)])

    def third_b(dx):
        ref = part_b(y, x_from(dx))
        to_sibling(ref)
        return out_row([remote(ref, ref, g3s.at[16 + dx * 4 + d], g3r.at[16 + dx * 4 + d], y_mate(d)) for d in (1, 3, 2)])

    flight.receive(keep_p)
    for copy in stage1[2:9]:
        flight.receive(copy)
    ref = part_a(y, x)
    second_a = out_row([remote(ref, ref, g2s.at[d], g2r.at[d], y_mate(d)) for d in range(1, 4)])
    ref = part_b(y, x)
    second_b = out_row([remote(ref, ref, g2s.at[3 + d], g2r.at[3 + d], x_mate(d)) for d in range(1, 4)])
    last_a, last_b = {0: third_a(0)}, {0: third_b(0)}
    for copy in second_c:
        flight.receive(copy)
    ref = go.at[:, z, :, half]
    last_c = out_row([remote(ref, ref, g3s.at[32 + d], g3r.at[32 + d], z_mate(d)) for d in (1, 7, 2, 6, 3, 5, 4)])
    to_sibling(ref)
    for d in (1, 3, 2):
        flight.receive(second_a[d - 1])
        last_a[d] = third_a(d)
        flight.receive(second_b[d - 1])
        last_b[d] = third_b(d)

    for copy in arrivals:
        flight.receive(copy)
    columns = dpr[...].reshape(2048, ROWS)
    for i in range(4):
        part = dot(wp[i * 256 : (i + 1) * 256, :], columns)
        dn[:, i * 256 : (i + 1) * 256] = part.T

    @pl.loop(0, ROWS // 16, unroll=2)
    def _(i):
        rows = pl.ds(pl.multiple_of(i * 16, 16), 16)
        values = hist[rows, :].astype(F32)
        centred = values - jnp.mean(values, axis=-1, keepdims=True)
        variance = jnp.mean(centred * centred, axis=-1, keepdims=True)
        scale = lax.rsqrt(variance + EPSILON)
        normed = centred * scale
        grad = dn[rows, :]
        one = jnp.mean(grad, axis=-1, keepdims=True)
        two = jnp.mean(grad * normed, axis=-1, keepdims=True)
        d_hist[rows, :] = (cot[rows, :].astype(F32) + scale * (grad - one - normed * two)).astype(BF16)

    for dj in (0, 1, 3, 2):
        for i, d in enumerate((1, 3, 2)):
            flight.receive(last_a[dj][i])
            to_sibling(part_a(y_from(dj), x_from(d)))
            flight.receive(last_b[dj][i])
            to_sibling(part_b(y_from(d), x_from(dj)))
    for copy, d in zip(last_c, (1, 7, 2, 6, 3, 5, 4)):
        flight.receive(copy)
        to_sibling(go.at[:, z_from(d), :, half])
    for copy in stage4:
        flight.receive(copy)
    flight.land()


def hand_over(rows_in, gp_in, go_in, rows, gp, go, rows_held, gp_held, go_held, get, put):
    steps = []
    for s in range(2):
        for i in range(4):
            at = (s, pl.ds(2 * i, 2))
            steps.append((gp_in.at[at], gp_held.at[at], gp.at[at]))
    for i in range(2):
        at = pl.ds(2 * i, 2)
        steps.append((go_in.at[at], go_held.at[at], go.at[at]))
    steps.append((rows_in, rows_held, rows))
    gets = [pltpu.make_async_copy(a, b, get.at[i]) for i, (a, b, _) in enumerate(steps)]
    puts = [pltpu.make_async_copy(b, c, put.at[i]) for i, (_, b, c) in enumerate(steps)]
    for copy in gets:
        copy.start()
    for first, second in zip(gets, puts):
        first.wait()
        second.start()
    for copy in puts:
        copy.wait()


def on_device(history, cotangent, lengths, w_proj, w_out):
    vmem, dma = pltpu.VMEM, pltpu.SemaphoreType.DMA
    whole = pl.BlockSpec(memory_space=vmem)
    anywhere = pl.BlockSpec(memory_space=pl.ANY)
    scratch = [
        vmem((ROWS, D), BF16),
        vmem((ROWS, D), BF16),
        vmem((EVENTS, D), BF16),
        vmem((EVENTS, D), BF16),
        vmem((EVENTS, D), BF16),
        vmem((D, 2048), BF16),
        vmem((512, D), BF16),
        vmem((HD, D), BF16),
        vmem((8, 128), jnp.int32),
        vmem((8, 128), jnp.int32),
        vmem((512, EVENTS), BF16),
        vmem((512, EVENTS), F32),
        vmem((EVENTS, HD), BF16),
        vmem((EVENTS, HD), BF16),
        vmem((EVENTS, EVENTS), BF16),
        vmem((EVENTS, EVENTS), F32),
        vmem((HD, EVENTS), F32),
        vmem((HD, EVENTS), F32),
        vmem((8, EVENTS), F32),
        vmem((4, 8, EVENTS), F32),
        vmem((HD, EVENTS), BF16),
        vmem((HD, EVENTS), BF16),
        vmem((HD, EVENTS), F32),
        vmem((HD, EVENTS), F32),
        vmem((4, HD, EVENTS), BF16),
        vmem((4, 4, HD, ROWS), BF16),
        vmem((4, 8, 80, HD), BF16),
        vmem((4, 8, 80, HD), BF16),
        vmem((8, 80, HD), BF16),
        vmem((8, 80, HD), BF16),
        vmem((2, 32, HD), BF16),
        vmem((16, HD), BF16),
        vmem((ROWS, D), F32),
        pltpu.SemaphoreType.REGULAR((3,)), dma((2,)), dma, dma, dma((2,)), dma((4,)),
        dma((4,)), dma((4,)), dma((4,)), dma((4,)), dma((4,)), dma((4,)), dma((4,)), dma((4,)), dma((4,)), dma((4,)),
        dma((8,)), dma((8,)), dma, dma((4,)), dma((4,)), dma((8,)), dma((8,)),
        dma((2,)), dma((11,)), dma((11,)), dma((10,)), dma((10,)), dma((40,)), dma((40,)), dma((40,)), dma((40,)),
    ]
    shapes = (
        jax.ShapeDtypeStruct((ROWS, D), BF16),
        jax.ShapeDtypeStruct((2, 8, 2, 32, 2048), BF16),
        jax.ShapeDtypeStruct((4, 8, 16, 1024), BF16),
    )
    results = pl.pallas_call(
        kernel,
        out_shape=shapes,
        in_specs=[anywhere, anywhere, whole, anywhere, anywhere],
        out_specs=(whole, anywhere, anywhere),
        scratch_shapes=scratch,
        compiler_params=pltpu.CompilerParams(
            collective_id=0, has_side_effects=True, vmem_limit_bytes=58 * 2**20
        ),
        name="layer",
    )(history[0], cotangent[0], lengths, w_proj, w_out)
    d_rows, grad_p, grad_o = pl.pallas_call(
        hand_over,
        out_shape=shapes,
        in_specs=[anywhere] * 3,
        out_specs=(anywhere,) * 3,
        scratch_shapes=[vmem(s.shape, s.dtype) for s in shapes] + [dma((11,)), dma((11,))],
        compiler_params=pltpu.CompilerParams(vmem_limit_bytes=58 * 2**20),
        name="hand_over",
    )(*results)
    return d_rows[None], grad_p.reshape(1024, 2048), grad_o.reshape(512, 1024)


def solution(mesh):
    in_specs = (P("dp", "ctx", None), P("dp", "ctx", None), P("dp", None), P(), P())
    out_specs = (P("dp", "ctx", None), P(), P())
    return jax.shard_map(
        on_device, mesh=mesh, in_specs=in_specs, out_specs=out_specs, check_vma=False
    )
```

time: 127 us -> 95.2 us (0.75)
  local copies, waits for them, and re-layouts: 19.8 us -> 0 us
  Pallas kernels: 106 us -> 94.4 us
    pallas_call x1 -> x2, Pallas kernels: 106 us -> 94.4 us  [the longest x1 89.5 us: on_device(): pl.pallas_call(kernel, out_shape=shapes, in_specs=[anywhere, anywhere, wh...]
    transpose x4 -> x0, local copies, waits for them, and re-layouts: 9.76 us -> none  [the longest x2 7.65 us: on_device(): grad_p = sheets[:, :, :, :512].transpose(0, 3, 2, 1, 4).reshape(1024, 2048)]
    reshape x2 -> x0, local copies, waits for them, and re-layouts: 9.33 us -> none  [the longest x1 7.78 us: on_device(): grad_p = sheets[:, :, :, :512].transpose(0, 3, 2, 1, 4).reshape(1024, 2048)]
where the time goes in v2:
time: 95.2 us; the launch traced here: 95.1 us
  Pallas kernels  94.4 us (99%)
    pallas_call x1, Pallas kernels, on_device(): pl.pallas_call(kernel, out_shape=shapes, in_specs=[anywhere, anywhere, wh...  89.5 us
    pallas_call x1, Pallas kernels, on_device(): pl.pallas_call(hand_over, out_shape=shapes, in_specs=[anywhere] * 3, out_...  4.89 us

profile of v2, /device:TPU:1, one launch (start us, length us, event | category | flops | bytes accessed | tf_op | source)
XLA Modules:
  0.0 95.1 jit_solution(13489425426211138036)
XLA Ops:
  0.6 89.5 %layer.1 = (bf16[128,1024]{1,0:T(8,128)(2,1)}, bf16[2,8,2,32,2048]{4,3,2,1,0:T(8,128)(2,1)}, bf16[4,8,16,1024]{3,2,1,0:T(8,128)(2,1)}) custom-call(bf16[128,1024]{1,0:T(8,128)(2,1)} %bitcast.5, bf16[128,1024]{1,0:T(8,128)(2,1)} %bitcast.6, s32[1,3]{1,0:T(1,128)} %lens.1, bf16[1024,2048]{1,0:T(8,128)(2,1)} %w_proj.1, bf16[512,1024]{1,0:T(8,128)(2,1)} %w_out.1), custom_call_target="tpu_custom_call" | custom-call | tf_op jit(solution)/shard_map/layer/pallas_call | solution.py:551
  90.2 4.9 %hand_over.1 = (bf16[128,1024]{1,0:T(8,128)(2,1)}, bf16[2,8,2,32,2048]{4,3,2,1,0:T(8,128)(2,1)}, bf16[4,8,16,1024]{3,2,1,0:T(8,128)(2,1)}) custom-call(bf16[128,1024]{1,0:T(8,128)(2,1)} %get-tuple-element.9.rows_in, bf16[2,8,2,32,2048]{4,3,2,1,0:T(8,128)(2,1)} %get-tuple-element.10.gp_in, bf16[4,8,16,1024]{3,2,1,0:T(8,128)(2,1)} %get-tuple-element.11.go_in), custom_call_target="tpu_custom_call" | custom-call | tf_op jit(solution)/shard_map/hand_over/pallas_call | solution.py:562

commit v3 on v2

--- a/solution.py
+++ b/solution.py
@@ -82,9 +82,9 @@
 
 def kernel(
     hist_in, cot_in, lens, w_proj, w_out, d_hist, gp, go,
-    hist, cot, xg, cg, xn, wp, wht, wo, lown, lsib, projt, spt, kr, vr, wm, sm, attnt, dgt, st, stx,
-    gt, dat, dkt, dvt, dpt, dpr, pay, ybuf, zsend, zbuf, piece_p, piece_o, dn,
-    known, insem, wsem, osem, lsem, swsem, xsem, xrsem, fsem, frsem, csem, crsem, gsem, grsem, stsem, strsem,
+    hist, cot, xg, cg, xn, wp, wht, wo, dgs, lown, lsib, projt, spt, kr, vr, wm, sm, attnt, dgt, st, stx,
+    gt, dat, dkt, dvt, dpt, dpr, pay, payo, ybuf, yobuf, zsend, zbuf, piece_p, piece_o, dn,
+    known, dgsem, dgrsem, dgfsem, insem, wsem, osem, lsem, swsem, xsem, xrsem, fsem, frsem, csem, crsem, gsem, grsem, stsem, strsem,
     asem, arsem, asem0, ysem, yrsem, zsem, zrsem, g0, g1s, g1r, g2s, g2r, g3s, g3r, g4s, g4r,
 ):
     dp, ctx = lax.axis_index("dp"), lax.axis_index("ctx")
@@ -117,13 +117,13 @@
     flight = Flight()
 
     get_w = pltpu.make_async_copy(w_proj, wp, wsem)
-    get_o = pltpu.make_async_copy(w_out.at[pl.ds(pl.multiple_of(x * HD, HD), HD), :], wo, osem)
+    get_o = pltpu.make_async_copy(w_out, wo, osem)
     get_x = pltpu.make_async_copy(hist_in, hist, insem.at[0])
     get_c = pltpu.make_async_copy(cot_in, cot, insem.at[1])
     flight.start_local(get_x)
     flight.start_local(get_c)
+    flight.start_local(get_o)
     flight.start_local(get_w)
-    flight.start_local(get_o)
 
     barrier = pltpu.get_barrier_semaphore()
     swap = device(x, 1 - yh, yl, z, 1 - c)
@@ -166,12 +166,24 @@
     def block_of(d, core):
         return pl.ds(pl.multiple_of((2 * x_from(d) + core) * ROWS, ROWS), ROWS)
 
-    push_x = [remote(xg.at[slot, :], xg.at[slot, :], xsem.at[d], xrsem.at[d], x_mate(d)) for d in range(1, 4)]
-    push_c = [remote(cg.at[slot, :], cg.at[slot, :], csem.at[d], crsem.at[d], x_mate(d)) for d in range(1, 4)]
+    def half_of(d, part):
+        return pl.ds(pl.multiple_of((2 * x_from(d) + c) * ROWS + part * (ROWS // 2), ROWS // 2), ROWS // 2)
+
+    push_x = {d: remote(xg.at[slot, :], xg.at[slot, :], xsem.at[d], xrsem.at[d], x_mate(d)) for d in (1, 3)}
+    push_c = {d: remote(cg.at[slot, :], cg.at[slot, :], csem.at[d], crsem.at[d], x_mate(d)) for d in (1, 3)}
+
+    def relay(ref, sends, receives, d):
+        part = half_of(d, d // 2)
+        return remote(ref.at[part, :], ref.at[part, :], sends.at[d - 1], receives.at[d - 1], x_mate(d))
+
+    relay_x = {d: relay(xg, xsem, xrsem, d) for d in (1, 3)}
+    relay_c = {d: relay(cg, csem, crsem, d) for d in (1, 3)}
     pass_x = [remote(xg.at[block_of(d, c), :], xg.at[block_of(d, c), :], fsem.at[d], frsem.at[d], sib) for d in range(4)]
-    pass_c = [remote(cg.at[block_of(d, c), :], cg.at[block_of(d, c), :], gsem.at[d], grsem.at[d], sib) for d in range(4)]
-    for copy in push_x:
-        flight.start(copy)
+    half = pl.ds(pl.multiple_of(c * 512, 512), 512)
+    rest = pl.ds(pl.multiple_of(512 - c * 512, 512), 512)
+    pass_c = [remote(cg.at[block_of(d, c), rest], cg.at[block_of(d, c), rest], gsem.at[d], grsem.at[d], sib) for d in range(4)]
+    for d in (1, 3):
+        flight.start(push_x[d])
     flight.start(pass_x[0])
 
     flight.receive(get_w)
@@ -179,10 +191,35 @@
         columns = pl.ds(pl.multiple_of(j * 512 + x * HD, HD), HD)
         wht[j * HD : (j + 1) * HD, :] = wp[:, columns].T
 
+    flight.receive(get_o)
+    for i in range(2):
+        dgs[i * PAIR : (i + 1) * PAIR, :] = dot_nt(wo[i * PAIR : (i + 1) * PAIR, :], cot[...]).astype(BF16)
+    hear(0)
+    tell(1)
+    at_block = pl.ds(pl.multiple_of((2 * x + yh) * ROWS, ROWS), ROWS)
+    for d in range(4):
+        head = lax.rem(x + d, 4)
+        source = dgs.at[pl.ds(pl.multiple_of(head * HD, HD), HD), :]
+        copy = remote(source, dgt.at[:, at_block], dgsem.at[d], dgrsem.at[d * 2 + yh], device(head, c, yl, z, c))
+        flight.start(copy, None if d else away, mirrored=False)
+
+    @pl.when(here)
+    def _():
+        dgt[:, at_block] = dgs[pl.ds(pl.multiple_of(x * HD, HD), HD), :]
+
+    graded = []
+    for d in range(4):
+        for row in range(2):
+            place = dgt.at[:, pl.ds(pl.multiple_of((2 * x_from(d) + row) * ROWS, ROWS), ROWS)]
+            copy = remote(place, place, dgsem.at[0], dgrsem.at[d * 2 + row], sib)
+            flight.expect(copy, copy.wait_recv, here if d else here & (yh != row))
+            graded.append(copy)
+    pass_g = remote(dgt, dgt, dgfsem.at[0], dgfsem.at[1], sib)
+
     def project(d):
         base = x_from(d) * PAIR
 
-        @pl.loop(0, PAIR // 16, unroll=4)
+        @pl.loop(0, PAIR // 16, unroll=8)
         def _(i):
             rows = pl.ds(pl.multiple_of(base + i * 16, 16), 16)
             values = xg[rows, :].astype(F32)
@@ -207,10 +244,9 @@
 
     flight.receive(pass_x[0])
     project(0)
-    hear(0)
-    tell(1)
     for d in (1, 3):
-        flight.receive(push_x[d - 1])
+        flight.receive(push_x[d])
+        flight.start(relay_x[d])
         flight.start(pass_x[d])
     flight.receive(swap_c)
 
@@ -218,15 +254,16 @@
     def _():
         cg[slot, :] = cot[...]
 
-    for copy in push_c:
-        flight.start(copy)
+    for d in (1, 3):
+        flight.start(push_c[d])
     flight.start(pass_c[0])
     for d in (1, 3):
         flight.receive(pass_x[d])
         project(d)
     hear(1)
     tell(2)
-    flight.receive(push_x[1])
+    for d in (1, 3):
+        flight.receive(relay_x[d])
     flight.start(pass_x[2])
     flight.receive(pass_x[2])
     project(2)
@@ -257,18 +294,15 @@
             total = term if total is None else total + term
         attnt[:, cols] = total
 
-    for d in (1, 3, 2):
-        flight.receive(push_c[d - 1])
-        flight.start(pass_c[d])
-    for d in range(4):
-        flight.receive(pass_c[d])
-    flight.receive(get_o)
-
+    for copy in graded:
+        flight.receive(copy)
+    flight.start(pass_g, here, mirrored=False)
+    flight.expect(pass_g, pass_g.wait_recv, away)
+    flight.receive(pass_g)
     st[4:8, :] = jnp.zeros((4, EVENTS), F32)
     for pb in range(4):
         cols = slice(pb * PAIR, (pb + 1) * PAIR)
-        d_gated = dot_nt(wo[...], cg[cols, :])
-        dgt[:, cols] = d_gated
+        d_gated = dgt[:, cols].astype(F32)
         attn = attnt[:, cols]
         g = d_gated * projt[0:HD, cols].astype(F32)
         average = jnp.mean(attn, axis=0, keepdims=True)
@@ -281,6 +315,10 @@
     push_s = [remote(st, stx.at[d], stsem.at[d], strsem.at[d], x_mate(d)) for d in range(1, 4)]
     for copy in push_s:
         flight.start(copy)
+    for d in (1, 3):
+        flight.receive(push_c[d])
+        flight.start(relay_c[d])
+        flight.start(pass_c[d])
     for copy in push_s:
         flight.receive(copy)
     parts = [st[...]] + [stx[d] for d in range(1, 4)]
@@ -293,7 +331,7 @@
     for pb in range(4):
         cols = slice(pb * PAIR, (pb + 1) * PAIR)
         u = projt[0:HD, cols].astype(F32)
-        d_gated = dgt[:, cols]
+        d_gated = dgt[:, cols].astype(F32)
         scale = a_scale[:, cols]
         a_norm = (attnt[:, cols] - average[:, cols]) * scale
         gt[:, cols] = (a_norm * u).astype(BF16)
@@ -322,22 +360,32 @@
     dpt[1] = (dvt[...] * spt[HD : 2 * HD, :]).astype(BF16)
     dpt[3] = (dkt[...] * SCALE * spt[3 * HD : 4 * HD, :]).astype(BF16)
 
-    half = pl.ds(pl.multiple_of(c * 512, 512), 512)
-    grad_o = dot(gt[...], cg[:, half]).astype(BF16)
-    for j in range(4):
-        pay[j, :, 64:80, :] = grad_o[:, j * HD : (j + 1) * HD].reshape(8, 16, HD)
     push_y = []
     for d in (1, 3, 2, 0):
         j = lax.rem(y + d, 4)
-        pay[j, :, 0:64, :] = dot(dpt[j], xn[:, half]).T.astype(BF16).reshape(8, 64, HD)
+        pay[j] = dot(dpt[j], xn[:, half]).T.astype(BF16).reshape(8, 64, HD)
         if d:
-            copy = remote(pay.at[j], ybuf.at[d], ysem.at[d], yrsem.at[d], y_mate(d))
-            flight.start(copy)
-            push_y.append(copy)
-    for copy in push_y:
-        flight.receive(copy)
-    zsend[...] = (
+            push_y.append(remote(pay.at[j], ybuf.at[d], ysem.at[d], yrsem.at[d], y_mate(d)))
+            flight.start(push_y[-1])
+    for d in (1, 3):
+        flight.receive(relay_c[d])
+    flight.start(pass_c[2])
+    for d in range(4):
+        flight.receive(pass_c[d])
+    grad_o = dot(gt[...], cg[:, half]).astype(BF16)
+    for j in range(4):
+        payo[j] = grad_o[:, j * HD : (j + 1) * HD].reshape(8, 16, HD)
+    push_o = []
+    for d in (1, 3, 2):
+        push_o.append(remote(payo.at[lax.rem(y + d, 4)], yobuf.at[d], ysem.at[3 + d], yrsem.at[3 + d], y_mate(d)))
+        flight.start(push_o[-1])
+    for copy in push_y + push_o:
+        flight.receive(copy)
+    zsend[:, 0:64, :] = (
         pay[y].astype(F32) + ybuf[1].astype(F32) + ybuf[2].astype(F32) + ybuf[3].astype(F32)
+    ).astype(BF16)
+    zsend[:, 64:80, :] = (
+        payo[y].astype(F32) + yobuf[1].astype(F32) + yobuf[2].astype(F32) + yobuf[3].astype(F32)
     ).astype(BF16)
     push_z = []
     for d in (1, 7, 2, 6, 3, 5, 4):
@@ -512,7 +560,8 @@
         vmem((EVENTS, D), BF16),
         vmem((D, 2048), BF16),
         vmem((512, D), BF16),
-        vmem((HD, D), BF16),
+        vmem((512, D), BF16),
+        vmem((512, ROWS), BF16),
         vmem((8, 128), jnp.int32),
         vmem((8, 128), jnp.int32),
         vmem((512, EVENTS), BF16),
@@ -522,7 +571,7 @@
         vmem((EVENTS, EVENTS), BF16),
         vmem((EVENTS, EVENTS), F32),
         vmem((HD, EVENTS), F32),
-        vmem((HD, EVENTS), F32),
+        vmem((HD, EVENTS), BF16),
         vmem((8, EVENTS), F32),
         vmem((4, 8, EVENTS), F32),
         vmem((HD, EVENTS), BF16),
@@ -531,16 +580,18 @@
         vmem((HD, EVENTS), F32),
         vmem((4, HD, EVENTS), BF16),
         vmem((4, 4, HD, ROWS), BF16),
-        vmem((4, 8, 80, HD), BF16),
-        vmem((4, 8, 80, HD), BF16),
+        vmem((4, 8, 64, HD), BF16),
+        vmem((4, 8, 16, HD), BF16),
+        vmem((4, 8, 64, HD), BF16),
+        vmem((4, 8, 16, HD), BF16),
         vmem((8, 80, HD), BF16),
         vmem((8, 80, HD), BF16),
         vmem((2, 32, HD), BF16),
         vmem((16, HD), BF16),
         vmem((ROWS, D), F32),
-        pltpu.SemaphoreType.REGULAR((3,)), dma((2,)), dma, dma, dma((2,)), dma((4,)),
+        pltpu.SemaphoreType.REGULAR((3,)), dma((4,)), dma((8,)), dma((2,)), dma((2,)), dma, dma, dma((2,)), dma((4,)),
         dma((4,)), dma((4,)), dma((4,)), dma((4,)), dma((4,)), dma((4,)), dma((4,)), dma((4,)), dma((4,)), dma((4,)),
-        dma((8,)), dma((8,)), dma, dma((4,)), dma((4,)), dma((8,)), dma((8,)),
+        dma((8,)), dma((8,)), dma, dma((8,)), dma((8,)), dma((8,)), dma((8,)),
         dma((2,)), dma((11,)), dma((11,)), dma((10,)), dma((10,)), dma((40,)), dma((40,)), dma((40,)), dma((40,)),
     ]
     shapes = (

time: 95.2 us -> 88.8 us (0.933)
  Pallas kernels: 94.4 us -> 88 us
    pallas_call x1, Pallas kernels: 89.5 us -> 83.2 us  [on_device(): pl.pallas_call(kernel, out_shape=shapes, in_specs=[anywhere, anywhere, wh...]
where the time goes in v3:
time: 88.8 us; the launch traced here: 88.7 us
  Pallas kernels  88 us (99%)
    pallas_call x1, Pallas kernels, on_device(): pl.pallas_call(kernel, out_shape=shapes, in_specs=[anywhere, anywhere, wh...  83.2 us
    pallas_call x1, Pallas kernels, on_device(): pl.pallas_call(hand_over, out_shape=shapes, in_specs=[anywhere] * 3, out_...  4.89 us

profile of v3, /device:TPU:1, one launch (start us, length us, event | category | flops | bytes accessed | tf_op | source)
XLA Modules:
  0.0 88.7 jit_solution(7403440357852476197)
XLA Ops:
  0.6 83.2 %layer.1 = (bf16[128,1024]{1,0:T(8,128)(2,1)}, bf16[2,8,2,32,2048]{4,3,2,1,0:T(8,128)(2,1)}, bf16[4,8,16,1024]{3,2,1,0:T(8,128)(2,1)}) custom-call(bf16[128,1024]{1,0:T(8,128)(2,1)} %bitcast.5, bf16[128,1024]{1,0:T(8,128)(2,1)} %bitcast.6, s32[1,3]{1,0:T(1,128)} %lens.1, bf16[1024,2048]{1,0:T(8,128)(2,1)} %w_proj.1, bf16[512,1024]{1,0:T(8,128)(2,1)} %w_out.1), custom_call_target="tpu_custom_call" | custom-call | tf_op jit(solution)/shard_map/layer/pallas_call | solution.py:602
  83.8 4.9 %hand_over.1 = (bf16[128,1024]{1,0:T(8,128)(2,1)}, bf16[2,8,2,32,2048]{4,3,2,1,0:T(8,128)(2,1)}, bf16[4,8,16,1024]{3,2,1,0:T(8,128)(2,1)}) custom-call(bf16[128,1024]{1,0:T(8,128)(2,1)} %get-tuple-element.9.rows_in, bf16[2,8,2,32,2048]{4,3,2,1,0:T(8,128)(2,1)} %get-tuple-element.10.gp_in, bf16[4,8,16,1024]{3,2,1,0:T(8,128)(2,1)} %get-tuple-element.11.go_in), custom_call_target="tpu_custom_call" | custom-call | tf_op jit(solution)/shard_map/hand_over/pallas_call | solution.py:613

commit v4 on v3

--- a/solution.py
+++ b/solution.py
@@ -132,11 +132,11 @@
         pl.semaphore_signal(barrier, inc=1, device_id=mate, device_id_type=MESH)
 
     def tell(level):
-        for mate in (sib, y_mate(2), z_mate(1), z_mate(7)):
+        for mate in (sib, swap, y_mate(2), z_mate(1), z_mate(7)):
             pl.semaphore_signal(known.at[level], inc=1, device_id=mate, device_id_type=MESH)
 
     def hear(level):
-        pl.semaphore_wait(known.at[level], 4)
+        pl.semaphore_wait(known.at[level], 5)
 
     lane = lax.broadcasted_iota(jnp.int32, (8, 128), 1)
     first = jnp.broadcast_to(lens[0:1, 0:1], (8, 128))
@@ -159,10 +159,6 @@
     def _():
         xg[slot, :] = hist[...]
 
-    flight.receive(swap_x)
-    flight.receive(get_c)
-    flight.start(swap_c, away)
-
     def block_of(d, core):
         return pl.ds(pl.multiple_of((2 * x_from(d) + core) * ROWS, ROWS), ROWS)
 
@@ -182,20 +178,32 @@
     half = pl.ds(pl.multiple_of(c * 512, 512), 512)
     rest = pl.ds(pl.multiple_of(512 - c * 512, 512), 512)
     pass_c = [remote(cg.at[block_of(d, c), rest], cg.at[block_of(d, c), rest], gsem.at[d], grsem.at[d], sib) for d in range(4)]
-    for d in (1, 3):
-        flight.start(push_x[d])
-    flight.start(pass_x[0])
+    far_x = remote(hist, xg.at[over, :], xsem.at[0], xrsem.at[0], device(lax.rem(x + 2, 4), 1 - yh, yl, z, 1 - c))
+
+    def first_pushes(when):
+        for copy in (push_x[1], push_x[3], pass_x[0]):
+            flight.start(copy, when, mirrored=False)
+
+    arrived_x = {}
+    for when, name in ((here, "here"), (away, "away")):
+        for d in (1, 3):
+            arrived_x[name, d] = object()
+            flight.expect(arrived_x[name, d], push_x[d].wait_recv, when)
+    flight.expect(pass_x[0], pass_x[0].wait_recv)
+    first_pushes(here)
 
     flight.receive(get_w)
     for j in range(4):
         columns = pl.ds(pl.multiple_of(j * 512 + x * HD, HD), HD)
         wht[j * HD : (j + 1) * HD, :] = wp[:, columns].T
 
+    flight.receive(get_c)
     flight.receive(get_o)
     for i in range(2):
         dgs[i * PAIR : (i + 1) * PAIR, :] = dot_nt(wo[i * PAIR : (i + 1) * PAIR, :], cot[...]).astype(BF16)
     hear(0)
     tell(1)
+    flight.start(far_x, away)
     at_block = pl.ds(pl.multiple_of((2 * x + yh) * ROWS, ROWS), ROWS)
     for d in range(4):
         head = lax.rem(x + d, 4)
@@ -242,12 +250,28 @@
             if j == 3:
                 kr[rows, :] = value.T
 
+    flight.receive(swap_x)
+    first_pushes(away)
+    flight.start(swap_c, away)
+    for d in (1, 3):
+        flight.receive(arrived_x["here", d])
+        flight.start(relay_x[d], here)
+        flight.start(pass_x[d], here, mirrored=False)
     flight.receive(pass_x[0])
     project(0)
     for d in (1, 3):
-        flight.receive(push_x[d])
-        flight.start(relay_x[d])
-        flight.start(pass_x[d])
+        flight.receive(arrived_x["away", d])
+        flight.start(pass_x[d], away, mirrored=False)
+        flight.expect(pass_x[d], pass_x[d].wait_recv)
+    hear(1)
+    tell(2)
+    for d in (1, 3):
+        flight.receive(pass_x[d])
+        project(d)
+    flight.receive(far_x)
+    for d in (1, 3):
+        flight.receive(relay_x[d])
+    flight.start(pass_x[2])
     flight.receive(swap_c)
 
     @pl.when(here)
@@ -257,14 +281,6 @@
     for d in (1, 3):
         flight.start(push_c[d])
     flight.start(pass_c[0])
-    for d in (1, 3):
-        flight.receive(pass_x[d])
-        project(d)
-    hear(1)
-    tell(2)
-    for d in (1, 3):
-        flight.receive(relay_x[d])
-    flight.start(pass_x[2])
     flight.receive(pass_x[2])
     project(2)
 
@@ -312,15 +328,15 @@
         st[2:3, cols] = jnp.sum(g, axis=0, keepdims=True)
         st[3:4, cols] = jnp.sum(g * centred, axis=0, keepdims=True)
 
-    push_s = [remote(st, stx.at[d], stsem.at[d], strsem.at[d], x_mate(d)) for d in range(1, 4)]
+    push_s = [remote(st, stx.at[d], stsem.at[d], strsem.at[d], x_mate(d)) for d in (2, 1, 3)]
     for copy in push_s:
         flight.start(copy)
+    for copy in push_s:
+        flight.receive(copy)
     for d in (1, 3):
         flight.receive(push_c[d])
         flight.start(relay_c[d])
         flight.start(pass_c[d])
-    for copy in push_s:
-        flight.receive(copy)
     parts = [st[...]] + [stx[d] for d in range(1, 4)]
     average = (parts[0][0:1] + parts[1][0:1] + parts[2][0:1] + parts[3][0:1]) * 0.25
     spread = sum(p[1:2] + HD * (p[0:1] - average) ** 2 for p in parts) * (1.0 / 512)
@@ -361,7 +377,7 @@
     dpt[3] = (dkt[...] * SCALE * spt[3 * HD : 4 * HD, :]).astype(BF16)
 
     push_y = []
-    for d in (1, 3, 2, 0):
+    for d in (2, 1, 3, 0):
         j = lax.rem(y + d, 4)
         pay[j] = dot(dpt[j], xn[:, half]).T.astype(BF16).reshape(8, 64, HD)
         if d:
@@ -376,7 +392,7 @@
     for j in range(4):
         payo[j] = grad_o[:, j * HD : (j + 1) * HD].reshape(8, 16, HD)
     push_o = []
-    for d in (1, 3, 2):
+    for d in (2, 1, 3):
         push_o.append(remote(payo.at[lax.rem(y + d, 4)], yobuf.at[d], ysem.at[3 + d], yrsem.at[3 + d], y_mate(d)))
         flight.start(push_o[-1])
     for copy in push_y + push_o:
@@ -388,7 +404,7 @@
         payo[y].astype(F32) + yobuf[1].astype(F32) + yobuf[2].astype(F32) + yobuf[3].astype(F32)
     ).astype(BF16)
     push_z = []
-    for d in (1, 7, 2, 6, 3, 5, 4):
+    for d in (4, 3, 5, 2, 6, 1, 7):
         copy = remote(zsend.at[lax.rem(z + d, 8)], zbuf.at[d], zsem.at[d], zrsem.at[d], z_mate(d))
         flight.start(copy)
         push_z.append(copy)
@@ -430,9 +446,9 @@
     keep_p = pltpu.make_async_copy(piece_p, own_p, g0.at[0])
     keep_o = pltpu.make_async_copy(piece_o, own_o, g0.at[1])
     stage1 = [keep_p, keep_o]
-    for d in (1, 7, 2, 6, 3, 5, 4):
+    for d in (4, 3, 5, 2, 6, 1, 7):
         stage1.append(remote(piece_p, own_p, g1s.at[d], g1r.at[d], z_mate(d)))
-    for d in range(1, 4):
+    for d in (2, 1, 3):
         stage1.append(remote(piece_o, own_o, g1s.at[7 + d], g1r.at[7 + d], y_mate(d)))
     flight.start_local(keep_p)
     flight.start_local(keep_o)
@@ -464,34 +480,75 @@
     ref = go.at[x, z, :, half]
     second_c = out_row([remote(ref, ref, g2s.at[6 + d], g2r.at[6 + d], x_mate(d)) for d in range(1, 4)])
 
-    def third_a(dj):
+    quarters = {1: pl.ds(0, 4), 3: pl.ds(4, 4)}
+    direct, relays = {}, {}
+
+    def third(dj):
         ref = part_a(y_from(dj), x)
         to_sibling(ref)
-        return out_row([remote(ref, ref, g3s.at[dj * 4 + d], g3r.at[dj * 4 + d], x_mate(d)) for d in (1, 3, 2)])
-
-    def third_b(dx):
-        ref = part_b(y, x_from(dx))
+        direct["a", dj] = {d: remote(ref, ref, g3s.at[dj * 4 + d], g3r.at[dj * 4 + d], x_mate(d)) for d in (1, 3)}
+        out_row(direct["a", dj].values())
+        ref = part_b(y, x_from(dj))
         to_sibling(ref)
-        return out_row([remote(ref, ref, g3s.at[16 + dx * 4 + d], g3r.at[16 + dx * 4 + d], y_mate(d)) for d in (1, 3, 2)])
+        direct["b", dj] = {d: remote(ref, ref, g3s.at[16 + dj * 4 + d], g3r.at[16 + dj * 4 + d], y_mate(d)) for d in (1, 3)}
+        out_row(direct["b", dj].values())
+
+    def pass_on(dj):
+        for name in ("a", "b"):
+            relays[name, dj] = []
+            for d in (1, 3):
+                flight.receive(direct[name, dj][d])
+                if name == "a":
+                    kind, head, row, at, mate = y_from(dj), x_from(d), 0, dj * 4 + d - 1, x_mate(d)
+                else:
+                    kind, head, row, at, mate = y_from(d), x_from(dj), 1, 16 + dj * 4 + d - 1, y_mate(d)
+                ref = gp.at[c, quarters[d], row, :, kind_at(kind, head)]
+                relays[name, dj].append(remote(ref, ref, g3s.at[at], g3r.at[at], mate))
+                flight.start(relays[name, dj][-1])
+            for d in (1, 3):
+                to_sibling(part_a(y_from(dj), x_from(d)) if name == "a" else part_b(y_from(d), x_from(dj)))
+
+    def finish(dj):
+        for name in ("a", "b"):
+            for copy in relays[name, dj]:
+                flight.receive(copy)
+            to_sibling(part_a(y_from(dj), x_from(2)) if name == "a" else part_b(y_from(2), x_from(dj)))
 
     flight.receive(keep_p)
     for copy in stage1[2:9]:
         flight.receive(copy)
     ref = part_a(y, x)
-    second_a = out_row([remote(ref, ref, g2s.at[d], g2r.at[d], y_mate(d)) for d in range(1, 4)])
+    second_a = {d: remote(ref, ref, g2s.at[d], g2r.at[d], y_mate(d)) for d in (2, 1, 3)}
+    out_row(second_a.values())
     ref = part_b(y, x)
-    second_b = out_row([remote(ref, ref, g2s.at[3 + d], g2r.at[3 + d], x_mate(d)) for d in range(1, 4)])
-    last_a, last_b = {0: third_a(0)}, {0: third_b(0)}
+    second_b = {d: remote(ref, ref, g2s.at[3 + d], g2r.at[3 + d], x_mate(d)) for d in (2, 1, 3)}
+    out_row(second_b.values())
+    third(0)
     for copy in second_c:
         flight.receive(copy)
     ref = go.at[:, z, :, half]
-    last_c = out_row([remote(ref, ref, g3s.at[32 + d], g3r.at[32 + d], z_mate(d)) for d in (1, 7, 2, 6, 3, 5, 4)])
+    last_c = {d: remote(ref, ref, g3s.at[32 + d], g3r.at[32 + d], z_mate(d)) for d in (2, 6, 1, 7)}
+    out_row(last_c.values())
     to_sibling(ref)
-    for d in (1, 3, 2):
-        flight.receive(second_a[d - 1])
-        last_a[d] = third_a(d)
-        flight.receive(second_b[d - 1])
-        last_b[d] = third_b(d)
+    for d in (1, 3):
+        flight.receive(second_a[d])
+        flight.receive(second_b[d])
+        third(d)
+    pass_on(0)
+    flight.receive(second_a[2])
+    flight.receive(second_b[2])
+    third(2)
+    relay_z = []
+    for d, near, at in ((2, 1, 4), (6, 7, 0)):
+        flight.receive(last_c[d])
+        ref = go.at[:, z_from(d), :, half]
+        part = go.at[pl.ds(0 if d == 2 else 2, 2), z_from(d), :, half]
+        relay_z.append(remote(ref, ref, g3s.at[32 + d + near - (8 if d == 6 else 0)], g3r.at[32 + d + near - (8 if d == 6 else 0)], z_mate(near)))
+        relay_z.append(remote(part, part, g3s.at[32 + at], g3r.at[32 + at], z_mate(d)))
+        out_row(relay_z[-2:])
+        to_sibling(ref)
+    pass_on(1)
+    pass_on(3)
 
     for copy in arrivals:
         flight.receive(copy)
@@ -500,6 +557,7 @@
         part = dot(wp[i * 256 : (i + 1) * 256, :], columns)
         dn[:, i * 256 : (i + 1) * 256] = part.T
 
+    pass_on(2)
     @pl.loop(0, ROWS // 16, unroll=2)
     def _(i):
         rows = pl.ds(pl.multiple_of(i * 16, 16), 16)
@@ -513,15 +571,16 @@
         two = jnp.mean(grad * normed, axis=-1, keepdims=True)
         d_hist[rows, :] = (cot[rows, :].astype(F32) + scale * (grad - one - normed * two)).astype(BF16)
 
-    for dj in (0, 1, 3, 2):
-        for i, d in enumerate((1, 3, 2)):
-            flight.receive(last_a[dj][i])
-            to_sibling(part_a(y_from(dj), x_from(d)))
-            flight.receive(last_b[dj][i])
-            to_sibling(part_b(y_from(d), x_from(dj)))
-    for copy, d in zip(last_c, (1, 7, 2, 6, 3, 5, 4)):
-        flight.receive(copy)
+    for d in (1, 7):
+        flight.receive(last_c[d])
         to_sibling(go.at[:, z_from(d), :, half])
+    finish(0)
+    for copy in relay_z:
+        flight.receive(copy)
+    for d in (3, 5, 4):
+        to_sibling(go.at[:, z_from(d), :, half])
+    for dj in (1, 3, 2):
+        finish(dj)
     for copy in stage4:
         flight.receive(copy)
     flight.land()
@@ -530,12 +589,8 @@
 def hand_over(rows_in, gp_in, go_in, rows, gp, go, rows_held, gp_held, go_held, get, put):
     steps = []
     for s in range(2):
-        for i in range(4):
-            at = (s, pl.ds(2 * i, 2))
-            steps.append((gp_in.at[at], gp_held.at[at], gp.at[at]))
-    for i in range(2):
-        at = pl.ds(2 * i, 2)
-        steps.append((go_in.at[at], go_held.at[at], go.at[at]))
+        steps.append((gp_in.at[s], gp_held.at[s], gp.at[s]))
+    steps.append((go_in, go_held, go))
     steps.append((rows_in, rows_held, rows))
     gets = [pltpu.make_async_copy(a, b, get.at[i]) for i, (a, b, _) in enumerate(steps)]
     puts = [pltpu.make_async_copy(b, c, put.at[i]) for i, (_, b, c) in enumerate(steps)]
@@ -615,7 +670,7 @@
         out_shape=shapes,
         in_specs=[anywhere] * 3,
         out_specs=(anywhere,) * 3,
-        scratch_shapes=[vmem(s.shape, s.dtype) for s in shapes] + [dma((11,)), dma((11,))],
+        scratch_shapes=[vmem(s.shape, s.dtype) for s in shapes] + [dma((4,)), dma((4,))],
         compiler_params=pltpu.CompilerParams(vmem_limit_bytes=58 * 2**20),
         name="hand_over",
     )(*results)

time: 88.8 us -> 86.4 us (0.973)
  Pallas kernels: 88 us -> 85.7 us
    pallas_call x1, Pallas kernels: 83.2 us -> 81.6 us  [on_device(): pl.pallas_call(kernel, out_shape=shapes, in_specs=[anywhere, anywhere, wh...]
where the time goes in v4:
time: 86.4 us; the launch traced here: 86.3 us
  Pallas kernels  85.7 us (99%)
    pallas_call x1, Pallas kernels, on_device(): pl.pallas_call(kernel, out_shape=shapes, in_specs=[anywhere, anywhere, wh...  81.6 us
    pallas_call x1, Pallas kernels, on_device(): pl.pallas_call(hand_over, out_shape=shapes, in_specs=[anywhere] * 3, out_...  4.06 us

profile of v4, /device:TPU:1, one launch (start us, length us, event | category | flops | bytes accessed | tf_op | source)
XLA Modules:
  0.0 86.3 jit_solution(5657040590332609956)
XLA Ops:
  0.6 81.6 %layer.1 = (bf16[128,1024]{1,0:T(8,128)(2,1)}, bf16[2,8,2,32,2048]{4,3,2,1,0:T(8,128)(2,1)}, bf16[4,8,16,1024]{3,2,1,0:T(8,128)(2,1)}) custom-call(bf16[128,1024]{1,0:T(8,128)(2,1)} %bitcast.5, bf16[128,1024]{1,0:T(8,128)(2,1)} %bitcast.6, s32[1,3]{1,0:T(1,128)} %lens.1, bf16[1024,2048]{1,0:T(8,128)(2,1)} %w_proj.1, bf16[512,1024]{1,0:T(8,128)(2,1)} %w_out.1), custom_call_target="tpu_custom_call" | custom-call | tf_op jit(solution)/shard_map/layer/pallas_call | solution.py:657
  82.3 4.1 %hand_over.1 = (bf16[128,1024]{1,0:T(8,128)(2,1)}, bf16[2,8,2,32,2048]{4,3,2,1,0:T(8,128)(2,1)}, bf16[4,8,16,1024]{3,2,1,0:T(8,128)(2,1)}) custom-call(bf16[128,1024]{1,0:T(8,128)(2,1)} %get-tuple-element.9.rows_in, bf16[2,8,2,32,2048]{4,3,2,1,0:T(8,128)(2,1)} %get-tuple-element.10.gp_in, bf16[4,8,16,1024]{3,2,1,0:T(8,128)(2,1)} %get-tuple-element.11.go_in), custom_call_target="tpu_custom_call" | custom-call | tf_op jit(solution)/shard_map/hand_over/pallas_call | solution.py:668

commit v5 on v4

--- a/solution.py
+++ b/solution.py
@@ -586,20 +586,12 @@
     flight.land()
 
 
-def hand_over(rows_in, gp_in, go_in, rows, gp, go, rows_held, gp_held, go_held, get, put):
-    steps = []
-    for s in range(2):
-        steps.append((gp_in.at[s], gp_held.at[s], gp.at[s]))
-    steps.append((go_in, go_held, go))
-    steps.append((rows_in, rows_held, rows))
-    gets = [pltpu.make_async_copy(a, b, get.at[i]) for i, (a, b, _) in enumerate(steps)]
-    puts = [pltpu.make_async_copy(b, c, put.at[i]) for i, (_, b, c) in enumerate(steps)]
-    for copy in gets:
+def hand_over(rows_in, gp_in, go_in, rows, gp, go, sems):
+    copies = [pltpu.make_async_copy(gp_in.at[s], gp.at[s], sems.at[s]) for s in range(2)]
+    copies += [pltpu.make_async_copy(go_in, go, sems.at[2]), pltpu.make_async_copy(rows_in, rows, sems.at[3])]
+    for copy in copies:
         copy.start()
-    for first, second in zip(gets, puts):
-        first.wait()
-        second.start()
-    for copy in puts:
+    for copy in copies:
         copy.wait()
 
 
@@ -661,7 +653,7 @@
         out_specs=(whole, anywhere, anywhere),
         scratch_shapes=scratch,
         compiler_params=pltpu.CompilerParams(
-            collective_id=0, has_side_effects=True, vmem_limit_bytes=58 * 2**20
+            collective_id=0, has_side_effects=True, vmem_limit_bytes=47 * 2**20
         ),
         name="layer",
     )(history[0], cotangent[0], lengths, w_proj, w_out)
@@ -670,8 +662,8 @@
         out_shape=shapes,
         in_specs=[anywhere] * 3,
         out_specs=(anywhere,) * 3,
-        scratch_shapes=[vmem(s.shape, s.dtype) for s in shapes] + [dma((4,)), dma((4,))],
-        compiler_params=pltpu.CompilerParams(vmem_limit_bytes=58 * 2**20),
+        scratch_shapes=[dma((4,))],
+        compiler_params=pltpu.CompilerParams(vmem_limit_bytes=4 * 2**20),
         name="hand_over",
     )(*results)
     return d_rows[None], grad_p.reshape(1024, 2048), grad_o.reshape(512, 1024)

time: 86.4 us -> 84.9 us (0.983)
  Pallas kernels: 85.7 us -> 80.3 us
  local copies, waits for them, and re-layouts: 0 us -> 3.77 us
    pallas_call x1, Pallas kernels: 81.6 us -> 77.8 us  [on_device(): pl.pallas_call(kernel, out_shape=shapes, in_specs=[anywhere, anywhere, wh...]
    unnamed x0 -> x8, local copies, waits for them, and re-layouts: none -> 3.77 us
    pallas_call x1, Pallas kernels: 4.06 us -> 2.44 us  [on_device(): pl.pallas_call(hand_over, out_shape=shapes, in_specs=[anywhere] * 3, out_...]
where the time goes in v5:
time: 84.9 us; the launch traced here: 84.7 us
  Pallas kernels  80.3 us (95%)
  local copies, waits for them, and re-layouts  3.77 us (4%)
    pallas_call x1, Pallas kernels, on_device(): pl.pallas_call(kernel, out_shape=shapes, in_specs=[anywhere, anywhere, wh...  77.8 us
    unnamed x8, local copies, waits for them, and re-layouts  3.77 us
    pallas_call x1, Pallas kernels, on_device(): pl.pallas_call(hand_over, out_shape=shapes, in_specs=[anywhere] * 3, out_...  2.44 us

profile of v5, /device:TPU:1, one launch (start us, length us, event | category | flops | bytes accessed | tf_op | source)
XLA Modules:
  0.0 84.7 jit_solution(6453104810539866192)
XLA Ops:
  0.6 0.0 copy-start
  0.6 1.2 %copy-done = bf16[512,1024]{1,0:T(8,128)(2,1)S(1)} copy-done((bf16[512,1024]{1,0:T(8,128)(2,1)S(1)}, bf16[512,1024]{1,0:T(8,128)(2,1)}, u32[]{:S(2)}) %copy-start) | copy-done | bytes 1048600
  1.9 0.0 copy-start.1
  1.9 0.9 %copy-done.1 = bf16[1,128,1024]{2,1,0:T(8,128)(2,1)S(1)} copy-done((bf16[1,128,1024]{2,1,0:T(8,128)(2,1)S(1)}, bf16[1,128,1024]{2,1,0:T(8,128)(2,1)}, u32[]{:S(2)}) %copy-start.1) | copy-done | bytes 262168
  2.8 0.0 copy-start.2
  2.8 0.9 %copy-done.2 = bf16[1,128,1024]{2,1,0:T(8,128)(2,1)S(1)} copy-done((bf16[1,128,1024]{2,1,0:T(8,128)(2,1)S(1)}, bf16[1,128,1024]{2,1,0:T(8,128)(2,1)}, u32[]{:S(2)}) %copy-start.2) | copy-done | bytes 262168
  3.8 0.0 copy-start.3
  3.8 0.7 copy-done.3
  4.4 77.8 %layer.1 = (bf16[128,1024]{1,0:T(8,128)(2,1)S(1)}, bf16[2,8,2,32,2048]{4,3,2,1,0:T(8,128)(2,1)S(1)}, bf16[4,8,16,1024]{3,2,1,0:T(8,128)(2,1)S(1)}) custom-call(bf16[128,1024]{1,0:T(8,128)(2,1)S(1)} %bitcast.5, bf16[128,1024]{1,0:T(8,128)(2,1)S(1)} %bitcast.6, s32[1,3]{1,0:T(1,128)S(1)} %copy-done.3, bf16[1024,2048]{1,0:T(8,128)(2,1)} %w_proj.1, ...), custom_call_target="tpu_custom_call" | custom-call | tf_op jit(solution)/shard_map/layer/pallas_call | solution.py:649
  82.2 2.4 %hand_over.1 = (bf16[128,1024]{1,0:T(8,128)(2,1)}, bf16[2,8,2,32,2048]{4,3,2,1,0:T(8,128)(2,1)}, bf16[4,8,16,1024]{3,2,1,0:T(8,128)(2,1)}) custom-call(bf16[128,1024]{1,0:T(8,128)(2,1)S(1)} %get-tuple-element.9.rows_in, bf16[2,8,2,32,2048]{4,3,2,1,0:T(8,128)(2,1)S(1)} %get-tuple-element.10.gp_in, bf16[4,8,16,1024]{3,2,1,0:T(8,128)(2,1)S(1)} %get-tuple-element.11.go_in), custom_call_target="tpu_custom_call" | custom-call | tf_op jit(solution)/shard_map/hand_over/pallas_call | solution.py:660
Async XLA Ops:
  0.6 1.2 %copy-start = (bf16[512,1024]{1,0:T(8,128)(2,1)S(1)}, bf16[512,1024]{1,0:T(8,128)(2,1)}, u32[]{:S(2)}) copy-start(bf16[512,1024]{1,0:T(8,128)(2,1)} %w_out.1) | copy-start | bytes 3145732
  1.9 0.9 %copy-start.1 = (bf16[1,128,1024]{2,1,0:T(8,128)(2,1)S(1)}, bf16[1,128,1024]{2,1,0:T(8,128)(2,1)}, u32[]{:S(2)}) copy-start(bf16[1,128,1024]{2,1,0:T(8,128)(2,1)} %param.5) | copy-start | bytes 786436
  2.8 0.9 %copy-start.2 = (bf16[1,128,1024]{2,1,0:T(8,128)(2,1)S(1)}, bf16[1,128,1024]{2,1,0:T(8,128)(2,1)}, u32[]{:S(2)}) copy-start(bf16[1,128,1024]{2,1,0:T(8,128)(2,1)} %param.6) | copy-start | bytes 786436
  3.8 0.7 copy-start.3

commit v6 on v5

--- a/solution.py
+++ b/solution.py
@@ -455,6 +455,26 @@
     for copy in stage1[2:]:
         flight.start(copy)
 
+    for copy in arrivals:
+        flight.receive(copy)
+    columns = dpr[...].reshape(2048, ROWS)
+    for i in range(4):
+        part = dot(wp[i * 256 : (i + 1) * 256, :], columns)
+        dn[:, i * 256 : (i + 1) * 256] = part.T
+
+    @pl.loop(0, ROWS // 16, unroll=2)
+    def _(i):
+        rows = pl.ds(pl.multiple_of(i * 16, 16), 16)
+        values = hist[rows, :].astype(F32)
+        centred = values - jnp.mean(values, axis=-1, keepdims=True)
+        variance = jnp.mean(centred * centred, axis=-1, keepdims=True)
+        scale = lax.rsqrt(variance + EPSILON)
+        normed = centred * scale
+        grad = dn[rows, :]
+        one = jnp.mean(grad, axis=-1, keepdims=True)
+        two = jnp.mean(grad * normed, axis=-1, keepdims=True)
+        d_hist[rows, :] = (cot[rows, :].astype(F32) + scale * (grad - one - normed * two)).astype(BF16)
+
     stage4 = []
 
     def to_sibling(ref):
@@ -550,27 +570,7 @@
     pass_on(1)
     pass_on(3)
 
-    for copy in arrivals:
-        flight.receive(copy)
-    columns = dpr[...].reshape(2048, ROWS)
-    for i in range(4):
-        part = dot(wp[i * 256 : (i + 1) * 256, :], columns)
-        dn[:, i * 256 : (i + 1) * 256] = part.T
-
     pass_on(2)
-    @pl.loop(0, ROWS // 16, unroll=2)
-    def _(i):
-        rows = pl.ds(pl.multiple_of(i * 16, 16), 16)
-        values = hist[rows, :].astype(F32)
-        centred = values - jnp.mean(values, axis=-1, keepdims=True)
-        variance = jnp.mean(centred * centred, axis=-1, keepdims=True)
-        scale = lax.rsqrt(variance + EPSILON)
-        normed = centred * scale
-        grad = dn[rows, :]
-        one = jnp.mean(grad, axis=-1, keepdims=True)
-        two = jnp.mean(grad * normed, axis=-1, keepdims=True)
-        d_hist[rows, :] = (cot[rows, :].astype(F32) + scale * (grad - one - normed * two)).astype(BF16)
-
     for d in (1, 7):
         flight.receive(last_c[d])
         to_sibling(go.at[:, z_from(d), :, half])

time: 84.9 us -> 86.2 us (1.015)
  Pallas kernels: 80.3 us -> 81.5 us
    pallas_call x1, Pallas kernels: 77.8 us -> 79.1 us  [on_device(): pl.pallas_call(kernel, out_shape=shapes, in_specs=[anywhere, anywhere, wh...]
where the time goes in v6:
time: 86.2 us; the launch traced here: 85.9 us
  Pallas kernels  81.5 us (95%)
  local copies, waits for them, and re-layouts  3.77 us (4%)
    pallas_call x1, Pallas kernels, on_device(): pl.pallas_call(kernel, out_shape=shapes, in_specs=[anywhere, anywhere, wh...  79.1 us
    unnamed x8, local copies, waits for them, and re-layouts  3.77 us
    pallas_call x1, Pallas kernels, on_device(): pl.pallas_call(hand_over, out_shape=shapes, in_specs=[anywhere] * 3, out_...  2.44 us

profile of v6, /device:TPU:1, one launch (start us, length us, event | category | flops | bytes accessed | tf_op | source)
XLA Modules:
  0.0 85.9 jit_solution(8944941296114331157)
XLA Ops:
  0.6 0.0 copy-start
  0.6 1.2 %copy-done = bf16[512,1024]{1,0:T(8,128)(2,1)S(1)} copy-done((bf16[512,1024]{1,0:T(8,128)(2,1)S(1)}, bf16[512,1024]{1,0:T(8,128)(2,1)}, u32[]{:S(2)}) %copy-start) | copy-done | bytes 1048600
  1.9 0.0 copy-start.1
  1.9 0.9 %copy-done.1 = bf16[1,128,1024]{2,1,0:T(8,128)(2,1)S(1)} copy-done((bf16[1,128,1024]{2,1,0:T(8,128)(2,1)S(1)}, bf16[1,128,1024]{2,1,0:T(8,128)(2,1)}, u32[]{:S(2)}) %copy-start.1) | copy-done | bytes 262168
  2.8 0.0 copy-start.2
  2.8 0.9 %copy-done.2 = bf16[1,128,1024]{2,1,0:T(8,128)(2,1)S(1)} copy-done((bf16[1,128,1024]{2,1,0:T(8,128)(2,1)S(1)}, bf16[1,128,1024]{2,1,0:T(8,128)(2,1)}, u32[]{:S(2)}) %copy-start.2) | copy-done | bytes 262168
  3.8 0.0 copy-start.3
  3.8 0.7 copy-done.3
  4.4 79.1 %layer.1 = (bf16[128,1024]{1,0:T(8,128)(2,1)S(1)}, bf16[2,8,2,32,2048]{4,3,2,1,0:T(8,128)(2,1)S(1)}, bf16[4,8,16,1024]{3,2,1,0:T(8,128)(2,1)S(1)}) custom-call(bf16[128,1024]{1,0:T(8,128)(2,1)S(1)} %bitcast.5, bf16[128,1024]{1,0:T(8,128)(2,1)S(1)} %bitcast.6, s32[1,3]{1,0:T(1,128)S(1)} %copy-done.3, bf16[1024,2048]{1,0:T(8,128)(2,1)} %w_proj.1, ...), custom_call_target="tpu_custom_call" | custom-call | tf_op jit(solution)/shard_map/layer/pallas_call | solution.py:649
  83.5 2.4 %hand_over.1 = (bf16[128,1024]{1,0:T(8,128)(2,1)}, bf16[2,8,2,32,2048]{4,3,2,1,0:T(8,128)(2,1)}, bf16[4,8,16,1024]{3,2,1,0:T(8,128)(2,1)}) custom-call(bf16[128,1024]{1,0:T(8,128)(2,1)S(1)} %get-tuple-element.9.rows_in, bf16[2,8,2,32,2048]{4,3,2,1,0:T(8,128)(2,1)S(1)} %get-tuple-element.10.gp_in, bf16[4,8,16,1024]{3,2,1,0:T(8,128)(2,1)S(1)} %get-tuple-element.11.go_in), custom_call_target="tpu_custom_call" | custom-call | tf_op jit(solution)/shard_map/hand_over/pallas_call | solution.py:660
Async XLA Ops:
  0.6 1.2 %copy-start = (bf16[512,1024]{1,0:T(8,128)(2,1)S(1)}, bf16[512,1024]{1,0:T(8,128)(2,1)}, u32[]{:S(2)}) copy-start(bf16[512,1024]{1,0:T(8,128)(2,1)} %w_out.1) | copy-start | bytes 3145732
  1.9 0.9 %copy-start.1 = (bf16[1,128,1024]{2,1,0:T(8,128)(2,1)S(1)}, bf16[1,128,1024]{2,1,0:T(8,128)(2,1)}, u32[]{:S(2)}) copy-start(bf16[1,128,1024]{2,1,0:T(8,128)(2,1)} %param.5) | copy-start | bytes 786436
  2.8 0.9 %copy-start.2 = (bf16[1,128,1024]{2,1,0:T(8,128)(2,1)S(1)}, bf16[1,128,1024]{2,1,0:T(8,128)(2,1)}, u32[]{:S(2)}) copy-start(bf16[1,128,1024]{2,1,0:T(8,128)(2,1)} %param.6) | copy-start | bytes 786436
  3.8 0.7 copy-start.3

commit v7 on v5

--- a/solution.py
+++ b/solution.py
@@ -83,7 +83,7 @@
 def kernel(
     hist_in, cot_in, lens, w_proj, w_out, d_hist, gp, go,
     hist, cot, xg, cg, xn, wp, wht, wo, dgs, lown, lsib, projt, spt, kr, vr, wm, sm, attnt, dgt, st, stx,
-    gt, dat, dkt, dvt, dpt, dpr, pay, payo, ybuf, yobuf, zsend, zbuf, piece_p, piece_o, dn,
+    gt, dat, dlm, dpt, dpr, pay, payo, ybuf, yobuf, zsend, zbuf, piece_p, piece_o, dn,
     known, dgsem, dgrsem, dgfsem, insem, wsem, osem, lsem, swsem, xsem, xrsem, fsem, frsem, csem, crsem, gsem, grsem, stsem, strsem,
     asem, arsem, asem0, ysem, yrsem, zsem, zrsem, g0, g1s, g1r, g2s, g2r, g3s, g3r, g4s, g4r,
 ):
@@ -356,25 +356,20 @@
 
     for pb in range(4):
         cols = slice(pb * PAIR, (pb + 1) * PAIR)
-        q = projt[2 * HD : 3 * HD, cols]
         da = dat[:, cols]
-        total = None
         for rb in range(pb, 4):
             rows = slice(rb * PAIR, (rb + 1) * PAIR)
-            d_logits = (dot(vr[rows, :], da) * sm[rows, cols]).astype(BF16)
-            term = dot(projt[3 * HD : 4 * HD, rows], d_logits)
-            total = term if total is None else total + term
-            d_key = dot_nt(q, d_logits)
-            d_value = dot_nt(da, wm[rows, cols])
-            if pb == 0:
-                dkt[:, rows] = d_key
-                dvt[:, rows] = d_value
-            else:
-                dkt[:, rows] += d_key
-                dvt[:, rows] += d_value
-        dpt[2, :, cols] = (total * SCALE * spt[2 * HD : 3 * HD, cols]).astype(BF16)
-    dpt[1] = (dvt[...] * spt[HD : 2 * HD, :]).astype(BF16)
-    dpt[3] = (dkt[...] * SCALE * spt[3 * HD : 4 * HD, :]).astype(BF16)
+            dlm[rows, cols] = (dot(vr[rows, :], da) * sm[rows, cols]).astype(BF16)
+        after = slice(pb * PAIR, EVENTS)
+        d_query = dot(projt[3 * HD : 4 * HD, after], dlm[after, cols])
+        dpt[2, :, cols] = (d_query * SCALE * spt[2 * HD : 3 * HD, cols]).astype(BF16)
+    for rb in range(4):
+        rows = slice(rb * PAIR, (rb + 1) * PAIR)
+        before = slice(0, (rb + 1) * PAIR)
+        d_value = dot_nt(dat[:, before], wm[rows, before])
+        d_key = dot_nt(projt[2 * HD : 3 * HD, before], dlm[rows, before])
+        dpt[1, :, rows] = (d_value * spt[HD : 2 * HD, rows]).astype(BF16)
+        dpt[3, :, rows] = (d_key * SCALE * spt[3 * HD : 4 * HD, rows]).astype(BF16)
 
     push_y = []
     for d in (2, 1, 3, 0):
@@ -623,8 +618,7 @@
         vmem((4, 8, EVENTS), F32),
         vmem((HD, EVENTS), BF16),
         vmem((HD, EVENTS), BF16),
-        vmem((HD, EVENTS), F32),
-        vmem((HD, EVENTS), F32),
+        vmem((EVENTS, EVENTS), BF16),
         vmem((4, HD, EVENTS), BF16),
         vmem((4, 4, HD, ROWS), BF16),
         vmem((4, 8, 64, HD), BF16),

time: 84.9 us -> 84.5 us (level)
  no operation moved by 1% of the time
where the time goes in v7:
time: 84.5 us; the launch traced here: 84.3 us
  Pallas kernels  79.8 us (94%)
  local copies, waits for them, and re-layouts  3.77 us (4%)
    pallas_call x1, Pallas kernels, on_device(): pl.pallas_call(kernel, out_shape=shapes, in_specs=[anywhere, anywhere, wh...  77.4 us
    unnamed x8, local copies, waits for them, and re-layouts  3.77 us
    pallas_call x1, Pallas kernels, on_device(): pl.pallas_call(hand_over, out_shape=shapes, in_specs=[anywhere] * 3, out_...  2.44 us

profile of v7, /device:TPU:1, one launch (start us, length us, event | category | flops | bytes accessed | tf_op | source)
XLA Modules:
  0.0 84.3 jit_solution(12519584783306772224)
XLA Ops:
  0.6 0.0 copy-start
  0.6 1.2 %copy-done = bf16[512,1024]{1,0:T(8,128)(2,1)S(1)} copy-done((bf16[512,1024]{1,0:T(8,128)(2,1)S(1)}, bf16[512,1024]{1,0:T(8,128)(2,1)}, u32[]{:S(2)}) %copy-start) | copy-done | bytes 1048600
  1.9 0.0 copy-start.1
  1.9 0.9 %copy-done.1 = bf16[1,128,1024]{2,1,0:T(8,128)(2,1)S(1)} copy-done((bf16[1,128,1024]{2,1,0:T(8,128)(2,1)S(1)}, bf16[1,128,1024]{2,1,0:T(8,128)(2,1)}, u32[]{:S(2)}) %copy-start.1) | copy-done | bytes 262168
  2.8 0.0 copy-start.2
  2.8 0.9 %copy-done.2 = bf16[1,128,1024]{2,1,0:T(8,128)(2,1)S(1)} copy-done((bf16[1,128,1024]{2,1,0:T(8,128)(2,1)S(1)}, bf16[1,128,1024]{2,1,0:T(8,128)(2,1)}, u32[]{:S(2)}) %copy-start.2) | copy-done | bytes 262168
  3.8 0.0 copy-start.3
  3.8 0.7 copy-done.3
  4.4 77.4 %layer.1 = (bf16[128,1024]{1,0:T(8,128)(2,1)S(1)}, bf16[2,8,2,32,2048]{4,3,2,1,0:T(8,128)(2,1)S(1)}, bf16[4,8,16,1024]{3,2,1,0:T(8,128)(2,1)S(1)}) custom-call(bf16[128,1024]{1,0:T(8,128)(2,1)S(1)} %bitcast.5, bf16[128,1024]{1,0:T(8,128)(2,1)S(1)} %bitcast.6, s32[1,3]{1,0:T(1,128)S(1)} %copy-done.3, bf16[1024,2048]{1,0:T(8,128)(2,1)} %w_proj.1, ...), custom_call_target="tpu_custom_call" | custom-call | tf_op jit(solution)/shard_map/layer/pallas_call | solution.py:643
  81.8 2.4 %hand_over.1 = (bf16[128,1024]{1,0:T(8,128)(2,1)}, bf16[2,8,2,32,2048]{4,3,2,1,0:T(8,128)(2,1)}, bf16[4,8,16,1024]{3,2,1,0:T(8,128)(2,1)}) custom-call(bf16[128,1024]{1,0:T(8,128)(2,1)S(1)} %get-tuple-element.9.rows_in, bf16[2,8,2,32,2048]{4,3,2,1,0:T(8,128)(2,1)S(1)} %get-tuple-element.10.gp_in, bf16[4,8,16,1024]{3,2,1,0:T(8,128)(2,1)S(1)} %get-tuple-element.11.go_in), custom_call_target="tpu_custom_call" | custom-call | tf_op jit(solution)/shard_map/hand_over/pallas_call | solution.py:654
Async XLA Ops:
  0.6 1.2 %copy-start = (bf16[512,1024]{1,0:T(8,128)(2,1)S(1)}, bf16[512,1024]{1,0:T(8,128)(2,1)}, u32[]{:S(2)}) copy-start(bf16[512,1024]{1,0:T(8,128)(2,1)} %w_out.1) | copy-start | bytes 3145732
  1.9 0.9 %copy-start.1 = (bf16[1,128,1024]{2,1,0:T(8,128)(2,1)S(1)}, bf16[1,128,1024]{2,1,0:T(8,128)(2,1)}, u32[]{:S(2)}) copy-start(bf16[1,128,1024]{2,1,0:T(8,128)(2,1)} %param.5) | copy-start | bytes 786436
  2.8 0.9 %copy-start.2 = (bf16[1,128,1024]{2,1,0:T(8,128)(2,1)S(1)}, bf16[1,128,1024]{2,1,0:T(8,128)(2,1)}, u32[]{:S(2)}) copy-start(bf16[1,128,1024]{2,1,0:T(8,128)(2,1)} %param.6) | copy-start | bytes 786436
  3.8 0.7 copy-start.3

commit v8 on v7

--- a/solution.py
+++ b/solution.py
@@ -294,7 +294,6 @@
         q = projt[2 * HD : 3 * HD, cols]
         p_at = lax.broadcasted_iota(jnp.int32, (1, PAIR), 1) + pb * PAIR
         p_end = jnp.where(p_at < first, first, jnp.where(p_at < second, second, EVENTS))
-        total = None
         for rb in range(pb, 4):
             rows = slice(rb * PAIR, (rb + 1) * PAIR)
             logits = dot(kr[rows, :], q) * SCALE
@@ -306,9 +305,8 @@
             weight = jnp.where(allowed, weight, 0.0).astype(BF16)
             wm[rows, cols] = weight
             sm[rows, cols] = jnp.where(allowed, slope, 0.0)
-            term = dot(projt[HD : 2 * HD, rows], weight)
-            total = term if total is None else total + term
-        attnt[:, cols] = total
+        after = slice(pb * PAIR, EVENTS)
+        attnt[:, cols] = dot(projt[HD : 2 * HD, after], wm[after, cols])
 
     for copy in graded:
         flight.receive(copy)

time: 84.5 us -> 84.4 us (level)
  no operation moved by 1% of the time
where the time goes in v8:
time: 84.4 us; the launch traced here: 84.2 us
  Pallas kernels  79.8 us (95%)
  local copies, waits for them, and re-layouts  3.77 us (4%)
    pallas_call x1, Pallas kernels, on_device(): pl.pallas_call(kernel, out_shape=shapes, in_specs=[anywhere, anywhere, wh...  77.3 us
    unnamed x8, local copies, waits for them, and re-layouts  3.77 us
    pallas_call x1, Pallas kernels, on_device(): pl.pallas_call(hand_over, out_shape=shapes, in_specs=[anywhere] * 3, out_...  2.44 us

profile of v8, /device:TPU:1, one launch (start us, length us, event | category | flops | bytes accessed | tf_op | source)
XLA Modules:
  0.0 84.2 jit_solution(829968662981144625)
XLA Ops:
  0.6 0.0 copy-start
  0.6 1.2 %copy-done = bf16[512,1024]{1,0:T(8,128)(2,1)S(1)} copy-done((bf16[512,1024]{1,0:T(8,128)(2,1)S(1)}, bf16[512,1024]{1,0:T(8,128)(2,1)}, u32[]{:S(2)}) %copy-start) | copy-done | bytes 1048600
  1.9 0.0 copy-start.1
  1.9 0.9 %copy-done.1 = bf16[1,128,1024]{2,1,0:T(8,128)(2,1)S(1)} copy-done((bf16[1,128,1024]{2,1,0:T(8,128)(2,1)S(1)}, bf16[1,128,1024]{2,1,0:T(8,128)(2,1)}, u32[]{:S(2)}) %copy-start.1) | copy-done | bytes 262168
  2.8 0.0 copy-start.2
  2.8 0.9 %copy-done.2 = bf16[1,128,1024]{2,1,0:T(8,128)(2,1)S(1)} copy-done((bf16[1,128,1024]{2,1,0:T(8,128)(2,1)S(1)}, bf16[1,128,1024]{2,1,0:T(8,128)(2,1)}, u32[]{:S(2)}) %copy-start.2) | copy-done | bytes 262168
  3.8 0.0 copy-start.3
  3.8 0.7 copy-done.3
  4.4 77.3 %layer.1 = (bf16[128,1024]{1,0:T(8,128)(2,1)S(1)}, bf16[2,8,2,32,2048]{4,3,2,1,0:T(8,128)(2,1)S(1)}, bf16[4,8,16,1024]{3,2,1,0:T(8,128)(2,1)S(1)}) custom-call(bf16[128,1024]{1,0:T(8,128)(2,1)S(1)} %bitcast.5, bf16[128,1024]{1,0:T(8,128)(2,1)S(1)} %bitcast.6, s32[1,3]{1,0:T(1,128)S(1)} %copy-done.3, bf16[1024,2048]{1,0:T(8,128)(2,1)} %w_proj.1, ...), custom_call_target="tpu_custom_call" | custom-call | tf_op jit(solution)/shard_map/layer/pallas_call | solution.py:641
  81.8 2.4 %hand_over.1 = (bf16[128,1024]{1,0:T(8,128)(2,1)}, bf16[2,8,2,32,2048]{4,3,2,1,0:T(8,128)(2,1)}, bf16[4,8,16,1024]{3,2,1,0:T(8,128)(2,1)}) custom-call(bf16[128,1024]{1,0:T(8,128)(2,1)S(1)} %get-tuple-element.9.rows_in, bf16[2,8,2,32,2048]{4,3,2,1,0:T(8,128)(2,1)S(1)} %get-tuple-element.10.gp_in, bf16[4,8,16,1024]{3,2,1,0:T(8,128)(2,1)S(1)} %get-tuple-element.11.go_in), custom_call_target="tpu_custom_call" | custom-call | tf_op jit(solution)/shard_map/hand_over/pallas_call | solution.py:652
Async XLA Ops:
  0.6 1.2 %copy-start = (bf16[512,1024]{1,0:T(8,128)(2,1)S(1)}, bf16[512,1024]{1,0:T(8,128)(2,1)}, u32[]{:S(2)}) copy-start(bf16[512,1024]{1,0:T(8,128)(2,1)} %w_out.1) | copy-start | bytes 3145732
  1.9 0.9 %copy-start.1 = (bf16[1,128,1024]{2,1,0:T(8,128)(2,1)S(1)}, bf16[1,128,1024]{2,1,0:T(8,128)(2,1)}, u32[]{:S(2)}) copy-start(bf16[1,128,1024]{2,1,0:T(8,128)(2,1)} %param.5) | copy-start | bytes 786436
  2.8 0.9 %copy-start.2 = (bf16[1,128,1024]{2,1,0:T(8,128)(2,1)S(1)}, bf16[1,128,1024]{2,1,0:T(8,128)(2,1)}, u32[]{:S(2)}) copy-start(bf16[1,128,1024]{2,1,0:T(8,128)(2,1)} %param.6) | copy-start | bytes 786436
  3.8 0.7 copy-start.3
